TPU v7x, 128 devices: a whole 4x4x4 slice. The times are simulated.
128 devices in a mesh: frame: 64 (over y, x, z_lo, core), tok: 2 (over z_hi).
Axes of the slice: x: 4, y: 4, z: 4 (z_hi: 2, z_lo: 2; z = z_hi * 2 + z_lo), core: 2. Of those that a mesh axis runs over, the one named last changes fastest.
Arguments:
- tokens: bfloat16 [32768, 1536], P(('frame', 'tok')), may hold values from -6 to 6
- modulation: float32 [64, 3, 1536], P('frame'), may hold values from -3 to 3
- qkv_weight: bfloat16 [3, 1536, 1536], P(None, None, 'tok'), may hold values from -1 to 1
- out_weight: bfloat16 [1536, 1536], P('tok'), may hold values from -0.15625 to 0.15625
- qk_gain: float32 [2, 1536], P(None, 'tok'), may hold values from 0.5 to 6
- text: bfloat16 [256, 1536], replicated, may hold values from -6 to 6
- text_count: int32 [1], replicated, may hold values from 64 to 256
- window: int32 [64, 2], P('frame'), may hold values from 0 to 64, as said below
Outputs:
- mixed: bfloat16 [32768, 1536], P(('frame', 'tok'))
Inputs may be any that keep to these rules, and one draw needn't show every extreme that they name: `window`: each row is f+1-8 <= start < end <= f+1 for frame f; the last frame has start = 56 and end = 64.
All inputs are finite; a program needn't handle non-finite values.
Results may differ from a plain program's by a relative error of at most 0.012.
The roundings to bfloat16 on the way count: a program that leaves them out, or rounds other values in their place, can miss the bound.
Values may be sent and summed in bfloat16 or wider, within the bound.
A program may use at most 128 MiB of HBM per device.

v0:
```python
import jax
import jax.numpy as jnp
from jax import lax
from jax.sharding import PartitionSpec as P

HEAD_DIM = 128
WIN = 8


EPSILON = 1e-06


def shifted(shard, axis, by):
    devices = lax.axis_size(axis)
    pairs = [(i, i + by) for i in range(devices) if 0 <= i + by < devices]
    return lax.ppermute(shard, axis, pairs)


def head_norm(projected, gain):
    shaped = projected.reshape(projected.shape[0], -1, HEAD_DIM)
    mean_square = jnp.mean(shaped * shaped, axis=-1, keepdims=True)
    return (shaped * lax.rsqrt(mean_square + EPSILON) * gain.reshape(1, -1, HEAD_DIM)).astype(
        jnp.bfloat16
    )


def modulate(rows, frame_mod):
    center = jnp.mean(rows, axis=-1, keepdims=True)
    spread = jnp.mean(jnp.square(rows - center), axis=-1, keepdims=True)
    normed = (rows - center) * lax.rsqrt(spread + EPSILON)
    return (normed * (1.0 + frame_mod[1]) + frame_mod[0]).astype(jnp.bfloat16)


def shards(tokens, modulation, qkv_weight, out_weight, qk_gain, text, text_count, window):
    frame_mod = modulation[0]
    hidden = modulate(tokens.astype(jnp.float32), frame_mod)
    triple = jnp.einsum(
        "td,cde->cte",
        lax.all_gather(hidden, "tok", axis=0, tiled=True),
        qkv_weight,
        preferred_element_type=jnp.float32,
    )
    frame_len = triple.shape[1]
    queries = head_norm(triple[0], qk_gain[0])
    own_keys = head_norm(triple[1], qk_gain[1])
    own_values = triple[2].reshape(frame_len, -1, HEAD_DIM).astype(jnp.bfloat16)
    local_heads = queries.shape[1]
    text_pair = jnp.einsum("td,cde->cte", text, qkv_weight[1:], preferred_element_type=jnp.float32)
    text_keys = head_norm(text_pair[0], qk_gain[1])
    text_values = text_pair[1].reshape(text.shape[0], -1, HEAD_DIM).astype(jnp.bfloat16)
    text_valid = jnp.arange(text.shape[0], dtype=jnp.int32) < text_count[0]
    scale = HEAD_DIM ** (-0.5)
    frame_id = lax.axis_index("frame")

    def block_valid(source):
        inside = (source >= window[0, 0]) & (source < window[0, 1])
        return jnp.full((frame_len,), inside)

    def absorb(running, key_block, value_block, valid):
        highest, total, accum = running
        scores = (
            jnp.einsum("qhd,khd->qhk", queries, key_block, preferred_element_type=jnp.float32)
            * scale
        )
        scores = jnp.where(valid[None, None, :], scores, -1e30)
        new_high = jnp.maximum(highest, jnp.max(scores, axis=-1))
        weights = jnp.exp(scores - new_high[..., None])
        shrink = jnp.exp(highest - new_high)
        total = total * shrink + jnp.sum(weights, axis=-1)
        accum = accum * shrink[..., None] + jnp.einsum(
            "qhk,khd->qhd",
            weights.astype(jnp.bfloat16),
            value_block,
            preferred_element_type=jnp.float32,
        )
        return (new_high, total, accum)

    running = (
        jnp.full((frame_len, local_heads), -1e30, jnp.float32),
        jnp.zeros((frame_len, local_heads), jnp.float32),
        jnp.zeros((frame_len, local_heads, HEAD_DIM), jnp.float32),
    )
    running = absorb(running, text_keys, text_values, text_valid)
    stacked = jnp.stack([own_keys, own_values], axis=0)
    running = absorb(running, own_keys, own_values, block_valid(frame_id))

    def relay_step(step, loop_state):
        moving, inner = loop_state
        moving = shifted(moving, "frame", 1)
        inner = absorb(inner, moving[0], moving[1], block_valid(frame_id - step))
        return (moving, inner)

    _, running = lax.fori_loop(1, WIN, relay_step, (stacked, running))
    highest, total, accum = running
    attended = (accum / total[..., None]).astype(jnp.bfloat16).reshape(frame_len, -1)
    update = lax.psum_scatter(
        jnp.dot(attended, out_weight, preferred_element_type=jnp.float32).astype(jnp.bfloat16),
        "tok",
        scatter_dimension=0,
        tiled=True,
    ).astype(jnp.float32)
    return (tokens.astype(jnp.float32) + frame_mod[2] * update).astype(jnp.bfloat16)


def solution(mesh):
    in_specs = (
        P(("frame", "tok"), None),
        P("frame", None, None),
        P(None, None, "tok"),
        P("tok", None),
        P(None, "tok"),
        P(),
        P(),
        P("frame", None),
    )
    out_specs = P(("frame", "tok"), None)
    return jax.shard_map(shards, mesh=mesh, in_specs=in_specs, out_specs=out_specs, check_vma=False)
```

profile of v0, /device:TPU:24, one launch (start us, length us, event | category | flops | bytes accessed | tf_op | source)
XLA Modules:
  0.0 377.4 jit_solution(3867694238937720790)
XLA Ops:
  11.5 4.0 %convolution_bitcast_fusion.1 = f32[2,256,768]{1,2,0:T(8,128)S(1)} fusion(bf16[3,1536,768]{2,1,0:T(8,128)(2,1)} %param.12, bf16[256,1536]{1,0:T(8,128)(2,1)} %param.15), kind=kOutput, calls=%fused_computation.65 | convolution fusion | flops 1207959552 | bytes 9437184 | tf_op jit(solution)/shard_map/td,cde->cte/dot_general | solution.py:48
  22.0 23.1 %all-gather.2.cloned.1.call-done = bf16[512,1536]{1,0:T(8,128)(2,1)} async-done(((bf16[256,1536]{1,0:T(8,128)(2,1)}), bf16[512,1536]{1,0:T(8,128)(2,1)}) %all-gather.2.cloned.1.call-update) | async-done | bytes 1572880 | tf_op jit(solution)/shard_map/all_gather | solution.py:39
  45.1 6.7 %convolution_bitcast_fusion = f32[3,512,768]{2,1,0:T(8,128)S(1)} fusion(bf16[3,1536,768]{2,1,0:T(8,128)(2,1)} %param.12, bf16[512,1536]{1,0:T(8,128)(2,1)} %all-gather.2.cloned.1.call-done), kind=kOutput, calls=%fused_computation.40 | convolution fusion | flops 3623878656 | bytes 13369344 | tf_op jit(solution)/shard_map/td,cde->cte/dot_general | solution.py:37
  54.9 3.0 copy.26
  62.5 3.0 copy.21
  69.7 2.6 copy.33
  72.3 3.0 bitcast_reduce_fusion.1
  80.4 2.2 bitcast_add_fusion.1
  82.5 3.0 copy.34
  85.6 248.8 %while.19 = (s32[]{:T(128)}, bf16[2,512,6,128]{3,1,2,0:T(8,128)(2,1)}, f32[512,6]{0,1:T(8,128)S(1)}, f32[512,6]{0,1:T(8,128)S(1)}, f32[512,6,128]{2,0,1:T(8,128)...) while((s32[]{:T(128)}, bf16[2,512,6,128]{3,1,2,0:T(8,128)(2,1)}, ...), condition=%wide.region_12.13_spmd, body=%wide.region_9.12_spmd.sunk | while | flops 823400448 | bytes 46596336 | solution.py:93
  85.6 1.9 collective-permute-start
  89.4 21.3 %collective-permute-done = bf16[2,512,6,128]{3,1,2,0:T(8,128)(2,1)} collective-permute-done((bf16[2,512,6,128]{3,1,2,0:T(8,128)(2,1)}, bf16[2,512,6,128]{3,1,2,0:T(8,128)(2,1)}, u32[]{:S(2)}, u32[]{:S(2)}) %collective-permute-start) | collective-permute-done | bytes 1572896 | tf_op jit(solution)/shard_map/while/body/eval_jaxpr/ppermute | solution.py:16
  110.6 2.1 bitcast_reduce_fusion.4
  114.0 2.8 copy.55
  116.8 3.1 bitcast_add_fusion.4
  121.1 1.9 collective-permute-start
  124.9 21.3 %collective-permute-done = bf16[2,512,6,128]{3,1,2,0:T(8,128)(2,1)} collective-permute-done((bf16[2,512,6,128]{3,1,2,0:T(8,128)(2,1)}, bf16[2,512,6,128]{3,1,2,0:T(8,128)(2,1)}, u32[]{:S(2)}, u32[]{:S(2)}) %collective-permute-start) | collective-permute-done | bytes 1572896 | tf_op jit(solution)/shard_map/while/body/eval_jaxpr/ppermute | solution.py:16
  146.2 2.1 bitcast_reduce_fusion.4
  149.6 2.8 copy.55
  152.4 3.1 bitcast_add_fusion.4
  156.6 1.9 collective-permute-start
  160.4 21.3 %collective-permute-done = bf16[2,512,6,128]{3,1,2,0:T(8,128)(2,1)} collective-permute-done((bf16[2,512,6,128]{3,1,2,0:T(8,128)(2,1)}, bf16[2,512,6,128]{3,1,2,0:T(8,128)(2,1)}, u32[]{:S(2)}, u32[]{:S(2)}) %collective-permute-start) | collective-permute-done | bytes 1572896 | tf_op jit(solution)/shard_map/while/body/eval_jaxpr/ppermute | solution.py:16
  181.7 2.1 bitcast_reduce_fusion.4
  185.1 2.8 copy.55
  187.9 3.1 bitcast_add_fusion.4
  192.2 1.9 collective-permute-start
  196.0 21.3 %collective-permute-done = bf16[2,512,6,128]{3,1,2,0:T(8,128)(2,1)} collective-permute-done((bf16[2,512,6,128]{3,1,2,0:T(8,128)(2,1)}, bf16[2,512,6,128]{3,1,2,0:T(8,128)(2,1)}, u32[]{:S(2)}, u32[]{:S(2)}) %collective-permute-start) | collective-permute-done | bytes 1572896 | tf_op jit(solution)/shard_map/while/body/eval_jaxpr/ppermute | solution.py:16
  217.2 2.1 bitcast_reduce_fusion.4
  220.7 2.8 copy.55
  223.4 3.1 bitcast_add_fusion.4
  227.7 1.9 collective-permute-start
  231.5 21.3 %collective-permute-done = bf16[2,512,6,128]{3,1,2,0:T(8,128)(2,1)} collective-permute-done((bf16[2,512,6,128]{3,1,2,0:T(8,128)(2,1)}, bf16[2,512,6,128]{3,1,2,0:T(8,128)(2,1)}, u32[]{:S(2)}, u32[]{:S(2)}) %collective-permute-start) | collective-permute-done | bytes 1572896 | tf_op jit(solution)/shard_map/while/body/eval_jaxpr/ppermute | solution.py:16
  252.8 2.1 bitcast_reduce_fusion.4
  256.2 2.8 copy.55
  259.0 3.1 bitcast_add_fusion.4
  263.3 1.9 collective-permute-start
  267.1 21.3 %collective-permute-done = bf16[2,512,6,128]{3,1,2,0:T(8,128)(2,1)} collective-permute-done((bf16[2,512,6,128]{3,1,2,0:T(8,128)(2,1)}, bf16[2,512,6,128]{3,1,2,0:T(8,128)(2,1)}, u32[]{:S(2)}, u32[]{:S(2)}) %collective-permute-start) | collective-permute-done | bytes 1572896 | tf_op jit(solution)/shard_map/while/body/eval_jaxpr/ppermute | solution.py:16
  288.3 2.1 bitcast_reduce_fusion.4
  291.7 2.8 copy.55
  294.5 3.1 bitcast_add_fusion.4
  302.6 21.3 %collective-permute-done = bf16[2,512,6,128]{3,1,2,0:T(8,128)(2,1)} collective-permute-done((bf16[2,512,6,128]{3,1,2,0:T(8,128)(2,1)}, bf16[2,512,6,128]{3,1,2,0:T(8,128)(2,1)}, u32[]{:S(2)}, u32[]{:S(2)}) %collective-permute-start) | collective-permute-done | bytes 1572896 | tf_op jit(solution)/shard_map/while/body/eval_jaxpr/ppermute | solution.py:16
  323.8 2.1 bitcast_reduce_fusion.4
  327.3 2.8 copy.55
  330.1 3.1 bitcast_add_fusion.4
  334.3 3.0 copy.36
  339.0 2.6 convolution_convert_fusion
  341.6 26.7 %reduce-scatter.2.cloned.1.call-done = bf16[256,1536]{1,0:T(8,128)(2,1)} async-done(((bf16[512,1536]{1,0:T(8,128)(2,1)}), bf16[256,1536]{1,0:T(8,128)(2,1)}) %reduce-scatter.2.cloned.1.call-update) | async-done | bytes 786448 | tf_op jit(solution)/shard_map/reduce_scatter | solution.py:96
  368.3 2.2 fusion.32
  (136 shorter events, 50.7 us)
Async XLA Ops:
  6.5 332.4 %copy-start = (bf16[768,1536]{1,0:T(8,128)(2,1)S(1)}, bf16[768,1536]{1,0:T(8,128)(2,1)}, u32[]{:S(2)}) copy-start(bf16[768,1536]{1,0:T(8,128)(2,1)} %param.13) | copy-start | bytes 7077892
  6.5 3.6 copy-start.3
  6.5 3.0 copy-start.18
  6.5 38.6 %all-gather.2.cloned.1.call-start = ((), (), s32[]{:S(2)}) async-start(), calls=%async_computation.1 | async-start | bytes 2359296 | tf_op jit(solution)/shard_map/all_gather | solution.py:39
  11.4 356.9 %reduce-scatter.2.cloned.1.call-start = ((), (), s32[]{:S(2)}) async-start(), calls=%async_computation.2 | async-start | bytes 2359296 | tf_op jit(solution)/shard_map/reduce_scatter | solution.py:96
  15.5 0.8 copy-start.12
  57.9 1.9 copy-start.2
  65.5 1.9 copy-start.1
  65.5 1.9 copy-start.14
  67.2 1.2 copy-start.8
  72.3 3.0 copy-start.5
  72.3 3.0 copy-start.10
  72.3 3.0 copy-start.15
  72.3 3.0 copy-start.16
  72.3 3.0 copy-start.19
  76.2 1.3 copy-start.9
  82.5 3.0 copy-start.11
  82.5 3.0 copy-start.13
  85.6 25.0 %collective-permute-start = (bf16[2,512,6,128]{3,1,2,0:T(8,128)(2,1)}, bf16[2,512,6,128]{3,1,2,0:T(8,128)(2,1)}, u32[]{:S(2)}, u32[]{:S(2)}) collective-permute-start(bf16[2,512,6,128]{3,1,2,0:T(8,128)(2,1)} %get-tuple-element.274), channel_id=1, source_target_pairs={{0,2},{2,4},{4,6},{6,8},{8,10},{10,12},{12,14},{14,16},{16,18},{18... | collective-permute-start | bytes 4718600 | tf_op jit(solution)/shard_map/while/body/eval_jaxpr/ppermute | solution.py:16
  114.0 2.8 copy-start.6
  120.0 1.1 copy-start.7
  121.1 25.0 %collective-permute-start = (bf16[2,512,6,128]{3,1,2,0:T(8,128)(2,1)}, bf16[2,512,6,128]{3,1,2,0:T(8,128)(2,1)}, u32[]{:S(2)}, u32[]{:S(2)}) collective-permute-start(bf16[2,512,6,128]{3,1,2,0:T(8,128)(2,1)} %get-tuple-element.274), channel_id=1, source_target_pairs={{0,2},{2,4},{4,6},{6,8},{8,10},{10,12},{12,14},{14,16},{16,18},{18... | collective-permute-start | bytes 4718600 | tf_op jit(solution)/shard_map/while/body/eval_jaxpr/ppermute | solution.py:16
  149.6 2.8 copy-start.6
  155.5 1.1 copy-start.7
  156.6 25.0 %collective-permute-start = (bf16[2,512,6,128]{3,1,2,0:T(8,128)(2,1)}, bf16[2,512,6,128]{3,1,2,0:T(8,128)(2,1)}, u32[]{:S(2)}, u32[]{:S(2)}) collective-permute-start(bf16[2,512,6,128]{3,1,2,0:T(8,128)(2,1)} %get-tuple-element.274), channel_id=1, source_target_pairs={{0,2},{2,4},{4,6},{6,8},{8,10},{10,12},{12,14},{14,16},{16,18},{18... | collective-permute-start | bytes 4718600 | tf_op jit(solution)/shard_map/while/body/eval_jaxpr/ppermute | solution.py:16
  185.1 2.8 copy-start.6
  191.0 1.1 copy-start.7
  192.2 25.0 %collective-permute-start = (bf16[2,512,6,128]{3,1,2,0:T(8,128)(2,1)}, bf16[2,512,6,128]{3,1,2,0:T(8,128)(2,1)}, u32[]{:S(2)}, u32[]{:S(2)}) collective-permute-start(bf16[2,512,6,128]{3,1,2,0:T(8,128)(2,1)} %get-tuple-element.274), channel_id=1, source_target_pairs={{0,2},{2,4},{4,6},{6,8},{8,10},{10,12},{12,14},{14,16},{16,18},{18... | collective-permute-start | bytes 4718600 | tf_op jit(solution)/shard_map/while/body/eval_jaxpr/ppermute | solution.py:16
  220.6 2.8 copy-start.6
  226.6 1.1 copy-start.7
  227.7 25.0 %collective-permute-start = (bf16[2,512,6,128]{3,1,2,0:T(8,128)(2,1)}, bf16[2,512,6,128]{3,1,2,0:T(8,128)(2,1)}, u32[]{:S(2)}, u32[]{:S(2)}) collective-permute-start(bf16[2,512,6,128]{3,1,2,0:T(8,128)(2,1)} %get-tuple-element.274), channel_id=1, source_target_pairs={{0,2},{2,4},{4,6},{6,8},{8,10},{10,12},{12,14},{14,16},{16,18},{18... | collective-permute-start | bytes 4718600 | tf_op jit(solution)/shard_map/while/body/eval_jaxpr/ppermute | solution.py:16
  256.2 2.8 copy-start.6
  262.1 1.1 copy-start.7
  263.3 25.0 %collective-permute-start = (bf16[2,512,6,128]{3,1,2,0:T(8,128)(2,1)}, bf16[2,512,6,128]{3,1,2,0:T(8,128)(2,1)}, u32[]{:S(2)}, u32[]{:S(2)}) collective-permute-start(bf16[2,512,6,128]{3,1,2,0:T(8,128)(2,1)} %get-tuple-element.274), channel_id=1, source_target_pairs={{0,2},{2,4},{4,6},{6,8},{8,10},{10,12},{12,14},{14,16},{16,18},{18... | collective-permute-start | bytes 4718600 | tf_op jit(solution)/shard_map/while/body/eval_jaxpr/ppermute | solution.py:16
  291.7 2.8 copy-start.6
  297.7 1.1 copy-start.7
  298.8 25.0 %collective-permute-start = (bf16[2,512,6,128]{3,1,2,0:T(8,128)(2,1)}, bf16[2,512,6,128]{3,1,2,0:T(8,128)(2,1)}, u32[]{:S(2)}, u32[]{:S(2)}) collective-permute-start(bf16[2,512,6,128]{3,1,2,0:T(8,128)(2,1)} %get-tuple-element.274), channel_id=1, source_target_pairs={{0,2},{2,4},{4,6},{6,8},{8,10},{10,12},{12,14},{14,16},{16,18},{18... | collective-permute-start | bytes 4718600 | tf_op jit(solution)/shard_map/while/body/eval_jaxpr/ppermute | solution.py:16
  327.3 2.8 copy-start.6
  333.2 1.1 copy-start.7
  341.6 26.7 %copy-start.4 = (bf16[256,1536]{1,0:T(8,128)(2,1)S(1)}, bf16[256,1536]{1,0:T(8,128)(2,1)}, u32[]{:S(2)}) copy-start(bf16[256,1536]{1,0:T(8,128)(2,1)} %param.10) | copy-start | bytes 2359300
  341.6 26.7 %copy-start.17 = (f32[1536]{0:T(1024)S(1)}, f32[1536]{0:T(1024)}, u32[]{:S(2)}) copy-start(f32[1536]{0:T(1024)} %get-tuple-element.163) | copy-start | bytes 18436
Sparse Core Ops, SparseCore 0:
  11.6 33.4 all-gather.1
  341.7 26.5 reduce-scatter.1
where the time goes:
time: 380 us; the launch traced here: 377 us
  waiting for transfers between devices  199 us (52%)
  matrix products  57.5 us (15%)
  local copies, waits for them, and re-layouts  55.2 us (15%)
  other arithmetic  27.5 us (7%)
  between operations  15.6 us (4%)
  starting transfers between devices  13.4 us (4%)
  loops' own time  9.59 us (3%)
    ppermute x7, waiting for transfers between devices, shifted(): return lax.ppermute(shard, axis, pairs)  149 us
    while x42, local copies, waits for them, and re-layouts  27.4 us
    reduce_scatter x1, waiting for transfers between devices, shards(): lax.psum_scatter(jnp.dot(attended, out_weight, preferred_element_type=jnp...  26.7 us
    dot_general x9, matrix products, absorb(): jnp.einsum('qhk,khd->qhd', weights.astype(jnp.bfloat16), value_block, pre...  25.6 us
    all_gather x1, waiting for transfers between devices, shards(): lax.all_gather(hidden, 'tok', axis=0, tiled=True)  23.1 us
    dot_general x9, matrix products, absorb(): jnp.einsum('qhd,khd->qhk', queries, key_block, preferred_element_type=jnp...  18.6 us
    ppermute x7, starting transfers between devices, shifted(): return lax.ppermute(shard, axis, pairs)  13.4 us
    reduce_sum x9, other arithmetic, absorb(): total = total * shrink + jnp.sum(weights, axis=-1)  10.7 us
  transfers between devices with their start and end apart: 9, of which 9 were waited for; matrix products, arithmetic and copies ran while one was open for 3% of the time, Pallas kernels for 0%

commit v1 on v0

v1 whole, which is shorter than its diff:
```python
import functools

import jax
import jax.numpy as jnp
from jax import lax
from jax.experimental import pallas as pl
from jax.experimental.pallas import tpu as pltpu
from jax.sharding import PartitionSpec as P

HEAD_DIM = 128
GROUP = 3
EPSILON = 1e-06
LOW = -1e30
SCALE = HEAD_DIM ** (-0.5) * 1.4426950408889634
MESH = pl.DeviceIdType.MESH


def dot(a, b):
    return jnp.dot(a, b, preferred_element_type=jnp.float32)


def dot_t(a, b):
    return lax.dot_general(a, b, (((1,), (1,)), ((), ())), preferred_element_type=jnp.float32)


def kernel(
    groups,
    tokens, mod, w_hbm, ow_hbm, gain, text, count, window,
    out,
    mine, hid, w, ow, kv, tk, q, acc, top, tot, att, attin,
    w_sem, hid_send, hid_relay, hid_recv, kv_send, kv_recv, ow_send, ow_recv, att_send, att_recv,
):
    rows, width = tokens.shape
    part_rows = mine.shape[0] // 2
    cols = GROUP * HEAD_DIM
    fi = lax.axis_index("frame")
    tok = lax.axis_index("tok")
    line = fi // 4
    zlo = (fi // 2) % 2
    core = fi % 2
    z = 2 * tok + zlo
    partner = 1 - core

    def dev(line_, z_, core_):
        return (4 * line_ + 2 * (z_ % 2) + core_, z_ // 2)

    def w_copy(c):
        return pltpu.make_async_copy(
            w_hbm.at[c, :, pl.ds(pl.multiple_of(zlo * cols, 128), cols)], w.at[c], w_sem.at[c]
        )

    def ow_copy():
        return pltpu.make_async_copy(ow_hbm, ow.at[tok], w_sem.at[3])

    for c in (1, 2, 0):
        w_copy(c).start()

    barrier = pltpu.get_barrier_semaphore()

    def greet(device):
        pl.semaphore_signal(barrier, inc=1, device_id=device, device_id_type=MESH)

    for c in range(2):
        for d in range(1, 4):
            greet(dev(line, (z + d) % 4, c))
    greet(dev(line, z, partner))

    @pl.when(line > 0)
    def _():
        for c in range(2):
            greet(dev(line - 1, z, c))

    @pl.when(line < groups - 1)
    def _():
        for c in range(2):
            greet(dev(line + 1, z, c))

    step_rows = 32

    def norm_rows(step, carry):
        at = pl.ds(pl.multiple_of(step * step_rows, step_rows), step_rows)
        x = tokens[at, :].astype(jnp.float32)
        center = jnp.mean(x, axis=-1, keepdims=True)
        x = x - center
        spread = jnp.mean(x * x, axis=-1, keepdims=True)
        x = x * lax.rsqrt(spread + EPSILON)
        mine[at, :] = (x * (1.0 + mod[0, 1:2, :]) + mod[0, 0:1, :]).astype(jnp.bfloat16)
        return carry

    lax.fori_loop(0, rows // step_rows, norm_rows, 0)
    mine[pl.ds(rows, 16), :] = jnp.full((16, width), window[0, 0], jnp.int32).astype(jnp.float32).astype(jnp.bfloat16)
    mine[pl.ds(rows + 16, 16), :] = jnp.full((16, width), window[0, 1], jnp.int32).astype(jnp.float32).astype(jnp.bfloat16)

    pl.semaphore_wait(barrier, 7 + jnp.where(line > 0, 2, 0) + jnp.where(line < groups - 1, 2, 0))

    def part_at(part):
        return pl.ds(pl.multiple_of(part * part_rows, 16), part_rows)

    def hid_copy(which, part):
        device = (dev(line, (z + 1) % 4, zlo), dev(line, (z + 3) % 4, zlo), dev(line, z, zlo))[which]
        return pltpu.make_async_remote_copy(
            src_ref=mine.at[part_at(part), :],
            dst_ref=hid.at[core, tok, part_at(part), :],
            send_sem=hid_send.at[which, part],
            recv_sem=hid_recv.at[core, tok, part],
            device_id=device,
            device_id_type=MESH,
        )

    hid_copy(0, 0).start()
    hid_copy(1, 1).start()
    hid_copy(0, 1).start()
    hid_copy(1, 0).start()

    @pl.when(core != zlo)
    def _():
        hid_copy(2, 0).start()
        hid_copy(2, 1).start()

    @pl.when(core == zlo)
    def _():
        hid[core, tok] = mine[...]

    def hid_wait(p, h, part):
        pltpu.make_async_remote_copy(
            src_ref=mine.at[part_at(part), :],
            dst_ref=hid.at[p, h, part_at(part), :],
            send_sem=hid_send.at[0, part],
            recv_sem=hid_recv.at[p, h, part],
            device_id=dev(line, z, partner),
            device_id_type=MESH,
        ).wait_recv()

    def hid_pass(p, h):
        part = jnp.where((2 * h + core + 1) % 4 == z, 0, 1)
        to = (z + 1 + 2 * part) % 4
        return pltpu.make_async_remote_copy(
            src_ref=hid.at[p, h, part_at(part), :],
            dst_ref=hid.at[p, h, part_at(part), :],
            send_sem=hid_relay.at[p, h],
            recv_sem=hid_recv.at[p, h, part],
            device_id=dev(line, to, core),
            device_id_type=MESH,
        )

    def kv_at(g, o, h):
        return kv.at[g, o, :, pl.ds(pl.multiple_of(h * rows, rows), rows), :]

    def kv_copy(kind, g, o, h, to_g, device):
        return pltpu.make_async_remote_copy(
            src_ref=kv_at(g, o, h),
            dst_ref=kv_at(to_g, o, h),
            send_sem=kv_send.at[kind, g, o, h],
            recv_sem=kv_recv.at[to_g, o, h],
            device_id=device,
            device_id_type=MESH,
        )

    def kv_wait(g, o, h):
        kv_copy(0, g, o, h, g, dev(line, z, partner)).wait_recv()

    def own_next(p, h):
        return kv_copy(0, 2, 2 * core + p, h, 1, dev(line + 1, z, core))

    def own_share(p, h):
        return kv_copy(1, 2, 2 * core + p, h, 2, dev(line, z, partner))

    def pass_next(p, h):
        o = 2 * core + p
        return kv_copy(0, 1, o, h, 0, dev(line + 1, z, jnp.where(o == 3, 1, 0)))

    def pass_share(p, h):
        return kv_copy(1, 1, 2 * core + p, h, 1, dev(line, z, partner))

    def old_share(h):
        return kv_copy(1, 0, 3, h, 0, dev(line, z, partner))

    has_prev = line > 0
    has_next = line < groups - 1

    def head_norm(x, which, hd):
        scaled = x * lax.rsqrt(jnp.mean(x * x, axis=-1, keepdims=True) + EPSILON)
        at = pl.ds(pl.multiple_of(zlo * cols + hd * HEAD_DIM, 128), HEAD_DIM)
        return (scaled * gain[which:which + 1, at]).astype(jnp.bfloat16)

    def block_of(k):
        return (core + k) % 2, (tok + k // 2) % 2

    def own_block(k, carry):
        p, h = block_of(k)

        @pl.when(jnp.logical_or(core != zlo, k > 0))
        def _():
            hid_wait(p, h, 0)
            hid_wait(p, h, 1)

            @pl.when(core != zlo)
            def _():
                hid_pass(p, h).start()

        x = hid[p, h, :rows, :]
        at = pl.ds(pl.multiple_of(h * rows, rows), rows)
        o = 2 * core + p
        keys = dot(x, w[1])
        values = dot(x, w[2])
        for hd in range(GROUP):
            lanes = slice(hd * HEAD_DIM, (hd + 1) * HEAD_DIM)
            kv[2, o, hd, at, :] = head_norm(keys[:, lanes], 1, hd)
            kv[2, o, GROUP + hd, at, :] = values[:, lanes].astype(jnp.bfloat16)

        @pl.when(has_next)
        def _():
            own_next(p, h).start()

        @pl.when(core == 0)
        def _():
            own_share(p, h).start()

        queries = dot(x, w[0])
        for hd in range(GROUP):
            lanes = slice(hd * HEAD_DIM, (hd + 1) * HEAD_DIM)
            q[p, hd, at, :] = head_norm(queries[:, lanes], 0, hd)
        return carry

    def pass_block(k, carry):
        p, h = block_of(k)

        @pl.when(has_prev)
        def _():
            kv_wait(1, 2 * core + p, h)

            @pl.when(jnp.logical_and(has_next, core + p > 0))
            def _():
                pass_next(p, h).start()

            pass_share(p, h).start()

        return carry

    for c in (1, 2, 0):
        w_copy(c).wait()
    ow_copy().start()
    lax.fori_loop(0, 2, own_block, 0)

    text_keys = dot(text[...], w[1])
    text_values = dot(text[...], w[2])
    for hd in range(GROUP):
        lanes = slice(hd * HEAD_DIM, (hd + 1) * HEAD_DIM)
        tk[hd] = head_norm(text_keys[:, lanes], 1, hd)
        tk[GROUP + hd] = text_values[:, lanes].astype(jnp.bfloat16)

    lax.fori_loop(0, 2, pass_block, 0)
    lax.fori_loop(2, 4, own_block, 0)

    def ow_cross():
        at = pl.ds(pl.multiple_of(core * cols, 128), cols)
        return pltpu.make_async_remote_copy(
            src_ref=ow.at[tok, at, :],
            dst_ref=ow.at[tok, at, :],
            send_sem=ow_send.at[0],
            recv_sem=ow_recv.at[0],
            device_id=dev(line, 3 - z, core),
            device_id_type=MESH,
        )

    def ow_share(which):
        at = pl.ds(pl.multiple_of(which * cols, 128), cols)
        return pltpu.make_async_remote_copy(
            src_ref=ow.at[1 - tok, at, :],
            dst_ref=ow.at[1 - tok, at, :],
            send_sem=ow_send.at[1],
            recv_sem=ow_recv.at[1],
            device_id=dev(line, z, partner),
            device_id_type=MESH,
        )

    def ow_wait_cross():
        at = pl.ds(pl.multiple_of(core * cols, 128), cols)
        pltpu.make_async_remote_copy(
            src_ref=ow.at[tok, at, :],
            dst_ref=ow.at[1 - tok, at, :],
            send_sem=ow_send.at[0],
            recv_sem=ow_recv.at[0],
            device_id=dev(line, 3 - z, core),
            device_id_type=MESH,
        ).wait_recv()

    ow_copy().wait()
    ow_cross().start()

    def text_attend(t, carry):
        p, hd = t // GROUP, t % GROUP
        s = dot_t(q[p, hd], tk[hd])
        s = jnp.where(lax.broadcasted_iota(jnp.int32, s.shape, 1) < count[0], s, LOW)
        m = jnp.broadcast_to(jnp.max(s, axis=1, keepdims=True) * SCALE, (2 * rows, HEAD_DIM))
        e = [jnp.exp2(s[:, n:n + HEAD_DIM] * SCALE - m) for n in range(0, s.shape[1], HEAD_DIM)]
        top[p, hd] = m
        tot[p, hd] = functools.reduce(jnp.add, e)
        acc[p, hd] = dot(jnp.concatenate([x.astype(jnp.bfloat16) for x in e], axis=1), tk[GROUP + hd])
        return carry

    def frame_attend(g, o):
        frame = (4 * (line - 2) + 4 * g + o).astype(jnp.float32)

        def step(t, carry):
            p, hd = t // GROUP, t % GROUP
            first = hid[p, 0, rows:rows + 16, :HEAD_DIM].astype(jnp.float32)[:1]
            end = hid[p, 0, rows + 16:rows + 32, :HEAD_DIM].astype(jnp.float32)[:1]
            inside = jnp.logical_and(frame >= first, frame < end)
            s = dot_t(q[p, hd], kv[g, o, hd])
            m = jnp.broadcast_to(jnp.max(s, axis=1, keepdims=True) * SCALE, (2 * rows, HEAD_DIM))
            before = top[p, hd]
            m = jnp.maximum(before, jnp.where(inside, m, LOW))
            top[p, hd] = m
            shrink = jnp.exp2(before - m)
            m = jnp.where(inside, m, -LOW)
            e = [jnp.exp2(s[:, n:n + HEAD_DIM] * SCALE - m) for n in range(0, s.shape[1], HEAD_DIM)]
            tot[p, hd] = tot[p, hd] * shrink + functools.reduce(jnp.add, e)
            acc[p, hd] = acc[p, hd] * shrink + dot(
                jnp.concatenate([x.astype(jnp.bfloat16) for x in e], axis=1), kv[g, o, GROUP + hd]
            )
            return carry

        return step

    lax.fori_loop(0, 2 * GROUP, text_attend, 0)
    lax.fori_loop(0, 2 * GROUP, frame_attend(2, 2 * core), 0)
    lax.fori_loop(2, 4, pass_block, 0)
    lax.fori_loop(GROUP, 2 * GROUP, frame_attend(2, 2 * core + 1), 0)

    def slot(j):
        s = 1 + 2 * core + j
        return s // 4, s % 4

    def slot_wait(g, o):
        @pl.when(jnp.logical_or(g != 1, o // 2 != core))
        def _():
            for h in range(2):
                half = h if h == 0 else 1
                kv_wait(g, o, half)

                @pl.when(jnp.logical_and(g == 0, core == 1))
                def _():
                    old_share(half).start()

    def older(i, carry):
        j = 6 - i
        g, o = slot(j)

        @pl.when(line + g >= 2)
        def _():
            slot_wait(g, o)
            lax.fori_loop(0, 2 * GROUP, frame_attend(g, o), 0)

        return carry

    lax.fori_loop(0, 6, older, 0)
    ow_wait_cross()
    ow_share(core).start()
    g0, o0 = slot(0)

    @pl.when(line >= 2)
    def _():
        slot_wait(g0, o0)
        lax.fori_loop(0, GROUP, frame_attend(g0, o0), 0)

    def att_copy(p, h):
        return pltpu.make_async_remote_copy(
            src_ref=att.at[p, h],
            dst_ref=attin.at[z],
            send_sem=att_send.at[p, h],
            recv_sem=att_recv.at[z],
            device_id=dev(line, 2 * h + core, p),
            device_id_type=MESH,
        )

    def is_here(p, h):
        return jnp.logical_and(2 * h + core == z, p == core)

    for p in range(2):
        for hd in range(GROUP):
            lanes = slice(hd * HEAD_DIM, (hd + 1) * HEAD_DIM)
            total = jnp.sum(tot[p, hd], axis=1, keepdims=True)
            result = (acc[p, hd] / total).astype(jnp.bfloat16)
            for h in range(2):
                att[p, h, :, lanes] = result[h * rows:(h + 1) * rows]
        for h in range(2):
            here = is_here(p, h)

            @pl.when(jnp.logical_not(here))
            def _():
                att_copy(p, h).start()

            @pl.when(here)
            def _():
                attin[z] = att[p, h]

    ow_share(partner).wait_recv()
    for s in range(4):
        @pl.when(jnp.logical_not(jnp.logical_and(s == z, core == zlo)))
        def _():
            pltpu.make_async_remote_copy(
                src_ref=att.at[0, 0],
                dst_ref=attin.at[s],
                send_sem=att_send.at[0, 0],
                recv_sem=att_recv.at[s],
                device_id=dev(line, z, partner),
                device_id_type=MESH,
            ).wait_recv()

    step_cols = 256

    def project(n, carry):
        at = pl.ds(pl.multiple_of(n * step_cols, step_cols), step_cols)
        update = dot(attin[0], ow[0, :cols, at])
        update += dot(attin[1], ow[0, cols:, at])
        update += dot(attin[2], ow[1, :cols, at])
        update += dot(attin[3], ow[1, cols:, at])
        out[:, at] = (tokens[:, at].astype(jnp.float32) + mod[0, 2:3, at] * update).astype(jnp.bfloat16)
        return carry

    lax.fori_loop(0, width // step_cols, project, 0)

    for part in range(2):
        hid_copy(0, part).wait_send()
        hid_copy(1, part).wait_send()

        @pl.when(core != zlo)
        def _():
            hid_copy(2, part).wait_send()

    ow_cross().wait_send()
    ow_share(core).wait_send()

    def drain(k, carry):
        p, h = k % 2, k // 2

        @pl.when(core != zlo)
        def _():
            hid_pass(p, h).wait_send()

        @pl.when(has_next)
        def _():
            own_next(p, h).wait_send()

        @pl.when(core == 0)
        def _():
            own_share(p, h).wait_send()

        @pl.when(has_prev)
        def _():
            @pl.when(jnp.logical_and(has_next, core + p > 0))
            def _():
                pass_next(p, h).wait_send()

            pass_share(p, h).wait_send()

        @pl.when(jnp.logical_not(is_here(p, h)))
        def _():
            att_copy(p, h).wait_send()

        @pl.when(jnp.logical_and(jnp.logical_and(line >= 2, core == 1), p == 0))
        def _():
            old_share(h).wait_send()

        return carry

    lax.fori_loop(0, 4, drain, 0)


def shards(groups, tokens, modulation, qkv_weight, out_weight, qk_gain, text, text_count, window):
    rows, width = tokens.shape
    text_rows = text.shape[0]
    cols = GROUP * HEAD_DIM
    bf16, f32 = jnp.bfloat16, jnp.float32
    vmem = pl.BlockSpec(memory_space=pltpu.VMEM)
    smem = pl.BlockSpec(memory_space=pltpu.SMEM)
    hbm = pl.BlockSpec(memory_space=pl.ANY)
    dma = pltpu.SemaphoreType.DMA
    return pl.pallas_call(
        functools.partial(kernel, groups),
        out_shape=jax.ShapeDtypeStruct((rows, width), bf16),
        in_specs=[vmem, vmem, hbm, hbm, vmem, vmem, smem, smem],
        out_specs=vmem,
        scratch_shapes=[
            pltpu.VMEM((rows + 32, width), bf16),
            pltpu.VMEM((2, 2, rows + 32, width), bf16),
            pltpu.VMEM((3, width, cols), bf16),
            pltpu.VMEM((2, width // 2, width), bf16),
            pltpu.VMEM((3, 4, 2 * GROUP, 2 * rows, HEAD_DIM), bf16),
            pltpu.VMEM((2 * GROUP, text_rows, HEAD_DIM), bf16),
            pltpu.VMEM((2, GROUP, 2 * rows, HEAD_DIM), bf16),
            pltpu.VMEM((2, GROUP, 2 * rows, HEAD_DIM), f32),
            pltpu.VMEM((2, GROUP, 2 * rows, HEAD_DIM), f32),
            pltpu.VMEM((2, GROUP, 2 * rows, HEAD_DIM), f32),
            pltpu.VMEM((2, 2, rows, cols), bf16),
            pltpu.VMEM((4, rows, cols), bf16),
            dma((4,)),
            dma((3, 2)),
            dma((2, 2)),
            dma((2, 2, 2)),
            dma((2, 3, 4, 2)),
            dma((3, 4, 2)),
            dma((2,)),
            dma((2,)),
            dma((2, 2)),
            dma((4,)),
        ],
        compiler_params=pltpu.CompilerParams(
            collective_id=0, has_side_effects=True, vmem_limit_bytes=58 * 1024 * 1024
        ),
        cost_estimate=pl.CostEstimate(flops=13_000_000_000, bytes_accessed=12_000_000, transcendentals=13_400_000),
    )(tokens, modulation, qkv_weight, out_weight, qk_gain, text, text_count, window)


def solution(mesh):
    in_specs = (
        P(("frame", "tok"), None),
        P("frame", None, None),
        P(None, None, "tok"),
        P("tok", None),
        P(None, "tok"),
        P(),
        P(),
        P("frame", None),
    )
    out_specs = P(("frame", "tok"), None)
    return jax.shard_map(
        functools.partial(shards, mesh.shape["frame"] // 4),
        mesh=mesh, in_specs=in_specs, out_specs=out_specs, check_vma=False,
    )
```

time: 380 us -> 119 us (0.31)
  waiting for transfers between devices: 199 us -> 0 us
  Pallas kernels: 0 us -> 112 us
  matrix products: 57.5 us -> 0 us
  local copies, waits for them, and re-layouts: 55.2 us -> 3.4 us
  other arithmetic: 27.5 us -> 0 us
  between operations: 15.6 us -> 0.66 us
  starting transfers between devices: 13.4 us -> 0 us
  loops' own time: 9.59 us -> 0 us
    ppermute x7 -> x0, waiting for transfers between devices: 149 us -> none  [shifted(): return lax.ppermute(shard, axis, pairs)]
    pallas_call x0 -> x1, Pallas kernels: none -> 112 us  [shards(): pl.pallas_call(functools.partial(kernel, groups), out_shape=jax.ShapeDtyp...]
    dot_general x21 -> x0, matrix products: 57.5 us -> none  [the longest x9 25.6 us: absorb(): jnp.einsum('qhk,khd->qhd', weights.astype(jnp.bfloat16), value_block, pre...]
    while x46 -> x0, local copies, waits for them, and re-layouts: 37.6 us -> none
    reduce_scatter x1 -> x0, waiting for transfers between devices: 26.7 us -> none  [shards(): lax.psum_scatter(jnp.dot(attended, out_weight, preferred_element_type=jnp...]
    all_gather x1 -> x0, waiting for transfers between devices: 23.1 us -> none  [shards(): lax.all_gather(hidden, 'tok', axis=0, tiled=True)]
    reduce_sum x14 -> x0, other arithmetic: 17.1 us -> none  [the longest x9 10.7 us: absorb(): total = total * shrink + jnp.sum(weights, axis=-1)]
    slice x15 -> x0, local copies, waits for them, and re-layouts: 14.2 us -> none  [the longest x3 6.25 us: shards(): queries = head_norm(triple[0], qk_gain[0])]
  transfers between devices with their start and end apart: 9 -> 0, of which waited for: 9 -> 0; matrix products, arithmetic and copies ran while one was open for 3% -> 0% of each run, Pallas kernels for 0% -> 0%
where the time goes in v1:
time: 119 us; the launch traced here: 116 us
  Pallas kernels  112 us (94%)
  local copies, waits for them, and re-layouts  3.4 us (3%)
    pallas_call x1, Pallas kernels, shards(): pl.pallas_call(functools.partial(kernel, groups), out_shape=jax.ShapeDtyp...  112 us
    unnamed x2, local copies, waits for them, and re-layouts  3.4 us

profile of v1, /device:TPU:24, one launch (start us, length us, event | category | flops | bytes accessed | tf_op | source)
XLA Modules:
  0.0 116.5 jit_solution(15348216104403094867)
XLA Ops:
  0.7 1.3 %copy.9.mod = f32[1,3,1536]{2,1,0:T(4,128)} copy(f32[1,3,1536]{2,0,1:T(1,128)} %param.9) | data formatting | bytes 36864 | tf_op args[1]
  2.0 112.4 %shard_map.82 = bf16[256,1536]{1,0:T(8,128)(2,1)} custom-call(bf16[256,1536]{1,0:T(8,128)(2,1)} %tokens.1, f32[1,3,1536]{2,1,0:T(4,128)} %copy.9.mod, bf16[3,1536,768]{2,1,0:T(8,128)(2,1)} %w_hbm.1, bf16[768,1536]{1,0:T(8,128)(2,1)} %ow_hbm.1, f32[2,768]{1,0:T(2,128)} %gain.1, bf16[256,1536]{1,0:T(8,128)(2,1)} %text.1, s32[1]{0:T(128)S(6)} %copy.11.count, ...), custom_call_target="tpu_custom_call" | custom-call | flops 12999999488 | bytes 12000000 | tf_op jit(solution)/shard_map/pallas_call | solution.py:480
  114.4 2.1 %copy.12 = bf16[256,1536]{1,0:T(8,128)(2,1)} copy(bf16[256,1536]{1,0:T(8,128)(2,1)} %shard_map.82) | data formatting | bytes 1572864

commit v2 on v1

v2 whole, which is shorter than its diff:
```python
import functools

import jax
import jax.numpy as jnp
from jax import lax
from jax.experimental import pallas as pl
from jax.experimental.pallas import tpu as pltpu
from jax.sharding import PartitionSpec as P

HEAD_DIM = 128
GROUP = 3
EPSILON = 1e-06
LOW = -1e30
SCALE = HEAD_DIM ** (-0.5) * 1.4426950408889634
MESH = pl.DeviceIdType.MESH


def dot(a, b):
    return jnp.dot(a, b, preferred_element_type=jnp.float32)


def dot_t(a, b):
    return lax.dot_general(a, b, (((1,), (1,)), ((), ())), preferred_element_type=jnp.float32)


def kernel(
    groups,
    tokens, mod, w_hbm, ow_hbm, gain, text, count, window,
    out,
    mine, hid, win_mine, win, w, ow, kv, tk, q, acc, top, tot, att, attin,
    w_sem, hid_send, hid_relay, hid_recv, win_send, win_recv, kv_send, kv_recv, ow_send, ow_recv, att_send, att_recv,
):
    rows, width = tokens.shape
    half = rows // 2
    cols = GROUP * HEAD_DIM
    depth = max(groups // 4, 1)
    fi = lax.axis_index("frame")
    tok = lax.axis_index("tok")
    line = fi // 4
    x = line % 4
    y = line // 4
    zlo = (fi // 2) % 2
    core = fi % 2
    z = 2 * tok + zlo
    partner = 1 - core
    near = core == zlo

    def dev(line_, z_, core_):
        return (4 * line_ + 2 * (z_ % 2) + core_, z_ // 2)

    def remote(src, dst, send, recv, device):
        return pltpu.make_async_remote_copy(
            src_ref=src, dst_ref=dst, send_sem=send, recv_sem=recv, device_id=device, device_id_type=MESH
        )

    beside = dev(line, z, partner)
    has_prev = line > 0
    has_next = line < groups - 1
    has_next2 = line < groups - 2
    back_line = jnp.where(x == 0, line + 3, line - 1)
    back_from = jnp.where(x == 3, line - 3, line + 1)
    has_back = jnp.logical_and(back_from >= 0, back_from < groups - 2)

    def w_copy(c):
        return pltpu.make_async_copy(
            w_hbm.at[c, :, pl.ds(pl.multiple_of(zlo * cols, 128), cols)], w.at[c], w_sem.at[c]
        )

    def ow_copy():
        return pltpu.make_async_copy(ow_hbm, ow.at[tok], w_sem.at[3])

    for c in (1, 2, 0):
        w_copy(c).start()

    barrier = pltpu.get_barrier_semaphore()

    def greet(device):
        pl.semaphore_signal(barrier, inc=1, device_id=device, device_id_type=MESH)

    for c in range(2):
        for d in range(1, 4):
            greet(dev(line, (z + d) % 4, c))
    greet(beside)

    for d in range(1, depth):
        greet(dev(4 * ((y + d) % depth) + x, z, core))

    def greet_line(line_):
        for c in range(2):
            greet(dev(line_, z, c))

    @pl.when(has_prev)
    def _():
        greet_line(line - 1)

    @pl.when(has_next)
    def _():
        greet_line(line + 1)

    @pl.when(has_next2)
    def _():
        greet(dev(back_line, z, core))

    @pl.when(has_back)
    def _():
        greet(dev(back_from, z, core))
        greet_line(back_from + 2)

    old_x = (line + 2) % 4
    old_relay = jnp.where(old_x == 0, line + 1, line - 3)

    @pl.when(line >= 2)
    def _():
        greet_line(old_relay)

    def ones(flag, n):
        return jnp.where(flag, n, 0)

    greeted = (
        7 + depth - 1 + ones(has_prev, 2) + ones(has_next, 2) + ones(has_next2, 1) + ones(has_back, 3) + ones(line >= 2, 2)
    )

    step_rows = 32

    def norm_rows(step, carry):
        at = pl.ds(pl.multiple_of(step * step_rows, step_rows), step_rows)
        v = tokens[at, :].astype(jnp.float32)
        v = v - jnp.mean(v, axis=-1, keepdims=True)
        spread = jnp.mean(v * v, axis=-1, keepdims=True)
        v = v * lax.rsqrt(spread + EPSILON)
        mine[at, :] = (v * (1.0 + mod[0, 1:2, :]) + mod[0, 0:1, :]).astype(jnp.bfloat16)
        return carry

    lax.fori_loop(0, rows // step_rows, norm_rows, 0)
    for n in range(2):
        win_mine[n] = jnp.full((8, HEAD_DIM), window[0, n], jnp.int32).astype(jnp.float32)

    pl.semaphore_wait(barrier, greeted)

    def half_at(part):
        return pl.ds(pl.multiple_of(part * half, half), half)

    def hid_copy(which, part):
        device = (dev(line, (z + 1) % 4, zlo), dev(line, (z + 3) % 4, zlo), dev(line, z, zlo))[which]
        return remote(
            mine.at[half_at(part), :], hid.at[core, tok, half_at(part), :],
            hid_send.at[which, part], hid_recv.at[core, tok, part], device,
        )

    def win_copy(which):
        device = (dev(line, (z + 1) % 4, zlo), dev(line, z, zlo))[which]
        return remote(win_mine, win.at[core], win_send.at[which], win_recv.at[core], device)

    def hid_wait(p, h, part):
        remote(
            mine.at[half_at(part), :], hid.at[p, h, half_at(part), :],
            hid_send.at[0, part], hid_recv.at[p, h, part], beside,
        ).wait_recv()

    def first_part(h):
        return jnp.where((2 * h + core + 1) % 4 == z, 0, 1)

    def hid_pass(p, h):
        part = first_part(h)
        return remote(
            hid.at[p, h, half_at(part), :], hid.at[p, h, half_at(part), :],
            hid_relay.at[p, h], hid_recv.at[p, h, part], dev(line, (z + 1 + 2 * part) % 4, core),
        )

    hid_copy(0, 0).start()
    hid_copy(1, 1).start()

    @pl.when(jnp.logical_not(near))
    def _():
        hid_copy(2, 0).start()
        hid_copy(2, 1).start()
        win_copy(1).start()

    win_copy(0).start()

    @pl.when(near)
    def _():
        hid[core, tok] = mine[...]
        win[core] = win_mine[...]

    def sub_rows(h, part):
        return pl.ds(pl.multiple_of((2 * h + part) * half, half), half)

    def kv_copy(kind, g, o, h, part, to_g, device):
        at = sub_rows(h, part)
        return remote(
            kv.at[g, o, :, at, :], kv.at[to_g, o, :, at, :],
            kv_send.at[kind, o, 2 * h + part], kv_recv.at[to_g, o, 2 * h + part], device,
        )

    def kv_wait(g, o, h, part):
        kv_copy(0, g, o, h, part, g, beside).wait_recv()

    def old_core(o):
        return jnp.where(o == 3, 1, 0)

    def own_next(o, h, part):
        return kv_copy(0, 2, o, h, part, 1, dev(line + 1, z, core))

    def own_back(o, h, part):
        return kv_copy(1, 2, o, h, part, 3, dev(back_line, z, core))

    def own_share(o, h, part):
        return kv_copy(2, 2, o, h, part, 2, beside)

    def pass_next(o, h, part):
        return kv_copy(3, 1, o, h, part, 0, dev(line + 1, z, old_core(o)))

    def pass_share(o, h, part):
        return kv_copy(4, 1, o, h, part, 1, beside)

    def pass_back(o, h, part):
        return kv_copy(5, 3, o, h, part, 0, dev(back_from + 2, z, old_core(o)))

    def old_share(h, part):
        return kv_copy(6, 0, 3, h, part, 0, beside)

    def sub_of(k):
        h = jnp.where(near, (tok + k // 4) % 2, k % 2)
        p = jnp.where(near, (core + k // 2) % 2, (k // 2) % 2)
        part = jnp.where(near, k % 2, (first_part(h) + k // 4) % 2)
        return p, h, part

    def by_next(k):
        return jnp.logical_and(k < 4, k % 2 == 0)

    def own_goes(k, o):
        return has_next, jnp.logical_and(jnp.logical_and(has_next2, o > 0), jnp.logical_not(by_next(k))), core == 0

    def pass_goes(k, o):
        return (
            jnp.logical_and(jnp.logical_and(has_prev, has_next), jnp.logical_and(o > 0, by_next(k))),
            jnp.logical_and(has_back, jnp.logical_and(o > 0, jnp.logical_not(by_next(k)))),
        )

    def head_norm(v, which, hd):
        scaled = v * lax.rsqrt(jnp.mean(v * v, axis=-1, keepdims=True) + EPSILON)
        at = pl.ds(pl.multiple_of(zlo * cols + hd * HEAD_DIM, 128), HEAD_DIM)
        return (scaled * gain[which:which + 1, at]).astype(jnp.bfloat16)

    def own_pair(kk, carry):
        subs = [sub_of(2 * kk), sub_of(2 * kk + 1)]
        p = subs[0][0]
        o = 2 * core + p
        for _, h, part in subs:
            @pl.when(jnp.logical_or(jnp.logical_not(near), kk > 0))
            def _():
                hid_wait(p, h, part)

                @pl.when(jnp.logical_and(jnp.logical_not(near), kk < 2))
                def _():
                    hid_pass(p, h).start()

        v = jnp.concatenate([hid[p, h, half_at(part), :] for _, h, part in subs], axis=0)
        keys = dot(v, w[1])
        values = dot(v, w[2])
        for hd in range(GROUP):
            lanes = slice(hd * HEAD_DIM, (hd + 1) * HEAD_DIM)
            normed = head_norm(keys[:, lanes], 1, hd)
            plain = values[:, lanes].astype(jnp.bfloat16)
            for n, (_, h, part) in enumerate(subs):
                kv[2, o, hd, sub_rows(h, part), :] = normed[n * half:(n + 1) * half]
                kv[2, o, GROUP + hd, sub_rows(h, part), :] = plain[n * half:(n + 1) * half]
        for n, (_, h, part) in enumerate(subs):
            for flag, copy in zip(own_goes(2 * kk + n, o), (own_next, own_back, own_share)):
                @pl.when(flag)
                def _():
                    copy(o, h, part).start()

        queries = dot(v, w[0])
        for hd in range(GROUP):
            lanes = slice(hd * HEAD_DIM, (hd + 1) * HEAD_DIM)
            normed = head_norm(queries[:, lanes], 0, hd)
            for n, (_, h, part) in enumerate(subs):
                q[p, hd, sub_rows(h, part), :] = normed[n * half:(n + 1) * half]
        return carry

    def pass_sub(k, carry):
        p, h, part = sub_of(k)
        o = 2 * core + p
        go_next, go_back = pass_goes(k, o)

        @pl.when(has_prev)
        def _():
            kv_wait(1, o, h, part)

            @pl.when(go_next)
            def _():
                pass_next(o, h, part).start()

            pass_share(o, h, part).start()

        @pl.when(go_back)
        def _():
            kv_wait(3, o, h, part)
            pass_back(o, h, part).start()

        return carry

    for c in (1, 2, 0):
        w_copy(c).wait()
    ow_copy().start()
    lax.fori_loop(0, 2, own_pair, 0)

    text_keys = dot(text[...], w[1])
    text_values = dot(text[...], w[2])
    for hd in range(GROUP):
        lanes = slice(hd * HEAD_DIM, (hd + 1) * HEAD_DIM)
        tk[hd] = head_norm(text_keys[:, lanes], 1, hd)
        tk[GROUP + hd] = text_values[:, lanes].astype(jnp.bfloat16)

    lax.fori_loop(0, 2, pass_sub, 0)
    hid_copy(0, 0).wait_send()
    hid_copy(1, 1).wait_send()
    hid_copy(0, 1).start()
    hid_copy(1, 0).start()
    lax.fori_loop(2, 4, pass_sub, 0)
    lax.fori_loop(2, 4, own_pair, 0)

    piece_rows = width // 2 // (2 * depth)

    def piece(n):
        return pl.ds(pl.multiple_of(n * piece_rows, 16), piece_rows)

    my_piece = 2 * y + core

    def ow_cross(which=None):
        of = tok if which is None else which
        return remote(
            ow.at[tok, piece(my_piece), :], ow.at[of, piece(my_piece), :],
            ow_send.at[0], ow_recv.at[my_piece], dev(line, 3 - z, core),
        )

    def ow_along(d):
        return remote(
            ow.at[1 - tok, piece(my_piece), :], ow.at[1 - tok, piece(my_piece), :],
            ow_send.at[d], ow_recv.at[my_piece], dev(4 * ((y + d) % depth) + x, z, core),
        )

    def ow_share(d, which):
        n = 2 * ((y + d) % depth) + which
        return remote(
            ow.at[1 - tok, piece(n), :], ow.at[1 - tok, piece(n), :],
            ow_send.at[depth + d], ow_recv.at[n], beside,
        )

    ow_copy().wait()
    ow_cross().start()

    @pl.when(near)
    def _():
        win_copy(0).wait_send()

    @pl.when(jnp.logical_not(near))
    def _():
        win_copy(0).wait_send()
        win_copy(1).wait_send()

    def win_wait(p):
        remote(win_mine, win.at[p], win_send.at[0], win_recv.at[p], beside).wait_recv()

    @pl.when(near)
    def _():
        win_wait(partner)

    @pl.when(jnp.logical_not(near))
    def _():
        win_wait(0)
        win_wait(1)

    def text_attend(t, carry):
        p, hd = t // GROUP, t % GROUP
        s = dot_t(q[p, hd], tk[hd])
        s = jnp.where(lax.broadcasted_iota(jnp.int32, s.shape, 1) < count[0], s, LOW)
        m = jnp.broadcast_to(jnp.max(s, axis=1, keepdims=True) * SCALE, (2 * rows, HEAD_DIM))
        e = [jnp.exp2(s[:, n:n + HEAD_DIM] * SCALE - m) for n in range(0, s.shape[1], HEAD_DIM)]
        top[p, hd] = m
        tot[p, hd] = functools.reduce(jnp.add, e)
        acc[p, hd] = dot(jnp.concatenate([v.astype(jnp.bfloat16) for v in e], axis=1), tk[GROUP + hd])
        return carry

    def frame_attend(g, o):
        frame = (4 * (line - 2) + 4 * g + o).astype(jnp.float32)

        def step(t, carry):
            p, hd = t // GROUP, t % GROUP
            inside = jnp.logical_and(frame >= win[p, 0, :1], frame < win[p, 1, :1])
            s = dot_t(q[p, hd], kv[g, o, hd])
            m = jnp.broadcast_to(jnp.max(s, axis=1, keepdims=True) * SCALE, (2 * rows, HEAD_DIM))
            before = top[p, hd]
            m = jnp.maximum(before, jnp.where(inside, m, LOW))
            top[p, hd] = m
            shrink = jnp.exp2(before - m)
            m = jnp.where(inside, m, -LOW)
            e = [jnp.exp2(s[:, n:n + HEAD_DIM] * SCALE - m) for n in range(0, s.shape[1], HEAD_DIM)]
            tot[p, hd] = tot[p, hd] * shrink + functools.reduce(jnp.add, e)
            acc[p, hd] = acc[p, hd] * shrink + dot(
                jnp.concatenate([v.astype(jnp.bfloat16) for v in e], axis=1), kv[g, o, GROUP + hd]
            )
            return carry

        return step

    lax.fori_loop(0, 2 * GROUP, text_attend, 0)
    pass_sub(4, 0)
    lax.fori_loop(0, GROUP, frame_attend(2, 2 * core), 0)
    pass_sub(5, 0)
    lax.fori_loop(GROUP, 2 * GROUP, frame_attend(2, 2 * core), 0)
    pass_sub(6, 0)
    lax.fori_loop(GROUP, 2 * GROUP, frame_attend(2, 2 * core + 1), 0)
    pass_sub(7, 0)

    def slot(j):
        s = 1 + 2 * core + j
        return s // 4, s % 4

    def slot_wait(g, o):
        for n in range(4):
            h, part = n // 2, n % 2
            kv_wait(g, o, h, part)

            @pl.when(jnp.logical_and(g == 0, core == 1))
            def _():
                old_share(h, part).start()

    def newer(i, carry):
        g, o = slot(6 - i)

        @pl.when(jnp.logical_and(g > 0, line + g >= 2))
        def _():
            @pl.when(jnp.logical_or(g != 1, o // 2 != core))
            def _():
                slot_wait(g, o)

            lax.fori_loop(0, 2 * GROUP, frame_attend(g, o), 0)

        return carry

    lax.fori_loop(0, 6, newer, 0)

    ow_cross(1 - tok).wait_recv()
    for d in range(1, depth):
        ow_along(d).start()
    ow_share(0, core).start()

    def att_copy(p, h):
        return remote(
            att.at[p, h], attin.at[z], att_send.at[p, h], att_recv.at[z], dev(line, 2 * h + core, p)
        )

    def is_here(p, h):
        return jnp.logical_and(2 * h + core == z, p == core)

    def finish(p):
        for hd in range(GROUP):
            lanes = slice(hd * HEAD_DIM, (hd + 1) * HEAD_DIM)
            total = jnp.sum(tot[p, hd], axis=1, keepdims=True)
            result = (acc[p, hd] / total).astype(jnp.bfloat16)
            for h in range(2):
                att[p, h, :, lanes] = result[h * rows:(h + 1) * rows]
        for h in range(2):
            here = is_here(p, h)

            @pl.when(jnp.logical_not(here))
            def _():
                att_copy(p, h).start()

            @pl.when(here)
            def _():
                attin[z] = att[p, h]

    for j in (2, 1):
        @pl.when(jnp.logical_and(line >= 2, core == 0))
        def _():
            g, o = 0, 1 + j
            slot_wait(g, o)
            lax.fori_loop(GROUP, 2 * GROUP, frame_attend(g, o), 0)

    finish(1)

    @pl.when(jnp.logical_and(line >= 2, core == 0))
    def _():
        slot_wait(0, 1)
        for o in (3, 2, 1):
            lax.fori_loop(0, GROUP, frame_attend(0, o), 0)

    @pl.when(jnp.logical_and(line >= 2, core == 1))
    def _():
        slot_wait(0, 3)
        lax.fori_loop(0, GROUP, frame_attend(0, 3), 0)

    finish(0)

    for d in range(1, depth):
        n = 2 * ((y + d) % depth) + core
        remote(
            ow.at[1 - tok, piece(n), :], ow.at[1 - tok, piece(n), :], ow_send.at[d], ow_recv.at[n], beside
        ).wait_recv()
        ow_share(d, core).start()
    for d in range(depth):
        ow_share(d, partner).wait_recv()

    for s in range(4):
        @pl.when(jnp.logical_not(jnp.logical_and(s == z, near)))
        def _():
            remote(att.at[0, 0], attin.at[s], att_send.at[0, 0], att_recv.at[s], beside).wait_recv()

    step_cols = 256

    def project(n, carry):
        at = pl.ds(pl.multiple_of(n * step_cols, step_cols), step_cols)
        update = dot(attin[0], ow[0, :cols, at])
        update += dot(attin[1], ow[0, cols:, at])
        update += dot(attin[2], ow[1, :cols, at])
        update += dot(attin[3], ow[1, cols:, at])
        out[:, at] = (tokens[:, at].astype(jnp.float32) + mod[0, 2:3, at] * update).astype(jnp.bfloat16)
        return carry

    lax.fori_loop(0, width // step_cols, project, 0)

    hid_copy(0, 1).wait_send()
    hid_copy(1, 0).wait_send()

    @pl.when(jnp.logical_not(near))
    def _():
        hid_copy(2, 0).wait_send()
        hid_copy(2, 1).wait_send()
        for p in range(2):
            for h in range(2):
                hid_pass(p, h).wait_send()

    ow_cross().wait_send()
    for d in range(1, depth):
        ow_along(d).wait_send()
    for d in range(depth):
        ow_share(d, core).wait_send()

    for p in range(2):
        for h in range(2):
            @pl.when(jnp.logical_not(is_here(p, h)))
            def _():
                att_copy(p, h).wait_send()

    def drain(k, carry):
        p, h, part = sub_of(k)
        o = 2 * core + p
        for flag, copy in zip(own_goes(k, o), (own_next, own_back, own_share)):
            @pl.when(flag)
            def _():
                copy(o, h, part).wait_send()

        for flag, copy in zip(pass_goes(k, o), (pass_next, pass_back)):
            @pl.when(flag)
            def _():
                copy(o, h, part).wait_send()

        @pl.when(has_prev)
        def _():
            pass_share(o, h, part).wait_send()

        @pl.when(jnp.logical_and(jnp.logical_and(line >= 2, core == 1), p == 0))
        def _():
            old_share(h, part).wait_send()

        return carry

    lax.fori_loop(0, 8, drain, 0)


def shards(groups, tokens, modulation, qkv_weight, out_weight, qk_gain, text, text_count, window):
    rows, width = tokens.shape
    text_rows = text.shape[0]
    cols = GROUP * HEAD_DIM
    depth = max(groups // 4, 1)
    bf16, f32 = jnp.bfloat16, jnp.float32
    vmem = pl.BlockSpec(memory_space=pltpu.VMEM)
    smem = pl.BlockSpec(memory_space=pltpu.SMEM)
    hbm = pl.BlockSpec(memory_space=pl.ANY)
    dma = pltpu.SemaphoreType.DMA
    return pl.pallas_call(
        functools.partial(kernel, groups),
        out_shape=jax.ShapeDtypeStruct((rows, width), bf16),
        in_specs=[vmem, vmem, hbm, hbm, vmem, vmem, smem, smem],
        out_specs=vmem,
        scratch_shapes=[
            pltpu.VMEM((rows, width), bf16),
            pltpu.VMEM((2, 2, rows, width), bf16),
            pltpu.VMEM((2, 8, HEAD_DIM), f32),
            pltpu.VMEM((2, 2, 8, HEAD_DIM), f32),
            pltpu.VMEM((3, width, cols), bf16),
            pltpu.VMEM((2, width // 2, width), bf16),
            pltpu.VMEM((4, 4, 2 * GROUP, 2 * rows, HEAD_DIM), bf16),
            pltpu.VMEM((2 * GROUP, text_rows, HEAD_DIM), bf16),
            pltpu.VMEM((2, GROUP, 2 * rows, HEAD_DIM), bf16),
            pltpu.VMEM((2, GROUP, 2 * rows, HEAD_DIM), f32),
            pltpu.VMEM((2, GROUP, 2 * rows, HEAD_DIM), f32),
            pltpu.VMEM((2, GROUP, 2 * rows, HEAD_DIM), f32),
            pltpu.VMEM((2, 2, rows, cols), bf16),
            pltpu.VMEM((4, rows, cols), bf16),
            dma((4,)),
            dma((3, 2)),
            dma((2, 2)),
            dma((2, 2, 2)),
            dma((2,)),
            dma((2,)),
            dma((7, 4, 4)),
            dma((4, 4, 4)),
            dma((2 * depth,)),
            dma((2 * depth,)),
            dma((2, 2)),
            dma((4,)),
        ],
        compiler_params=pltpu.CompilerParams(
            collective_id=0, has_side_effects=True, vmem_limit_bytes=58 * 1024 * 1024
        ),
        cost_estimate=pl.CostEstimate(flops=13_000_000_000, bytes_accessed=12_000_000, transcendentals=13_400_000),
    )(tokens, modulation, qkv_weight, out_weight, qk_gain, text, text_count, window)


def solution(mesh):
    in_specs = (
        P(("frame", "tok"), None),
        P("frame", None, None),
        P(None, None, "tok"),
        P("tok", None),
        P(None, "tok"),
        P(),
        P(),
        P("frame", None),
    )
    out_specs = P(("frame", "tok"), None)
    return jax.shard_map(
        functools.partial(shards, mesh.shape["frame"] // 4),
        mesh=mesh, in_specs=in_specs, out_specs=out_specs, check_vma=False,
    )
```

time: 119 us -> 120 us (level)
  the two profiles are of different devices: /device:TPU:24 before, /device:TPU:8 now
where the time goes in v2:
time: 120 us
  Pallas kernels  116 us (97%)
  local copies, waits for them, and re-layouts  3.4 us (3%)
    pallas_call x1, Pallas kernels, shards(): pl.pallas_call(functools.partial(kernel, groups), out_shape=jax.ShapeDtyp...  116 us
    unnamed x2, local copies, waits for them, and re-layouts  3.4 us

profile of v2, /device:TPU:8, one launch (start us, length us, event | category | flops | bytes accessed | tf_op | source)
XLA Modules:
  0.0 119.6 jit_solution(14866556181247231656)
XLA Ops:
  0.7 1.3 %copy.9.mod = f32[1,3,1536]{2,1,0:T(4,128)} copy(f32[1,3,1536]{2,0,1:T(1,128)} %param.9) | data formatting | bytes 36864 | tf_op args[1]
  2.0 115.5 %shard_map.82 = bf16[256,1536]{1,0:T(8,128)(2,1)} custom-call(bf16[256,1536]{1,0:T(8,128)(2,1)} %tokens.1, f32[1,3,1536]{2,1,0:T(4,128)} %copy.9.mod, bf16[3,1536,768]{2,1,0:T(8,128)(2,1)} %w_hbm.1, bf16[768,1536]{1,0:T(8,128)(2,1)} %ow_hbm.1, f32[2,768]{1,0:T(2,128)} %gain.1, bf16[256,1536]{1,0:T(8,128)(2,1)} %text.1, s32[1]{0:T(128)S(6)} %copy.11.count, ...), custom_call_target="tpu_custom_call" | custom-call | flops 12999999488 | bytes 12000000 | tf_op jit(solution)/shard_map/pallas_call | solution.py:585
  117.5 2.1 %copy.12 = bf16[256,1536]{1,0:T(8,128)(2,1)} copy(bf16[256,1536]{1,0:T(8,128)(2,1)} %shard_map.82) | data formatting | bytes 1572864

commit v3 on v2

--- a/solution.py
+++ b/solution.py
@@ -57,8 +57,8 @@
     has_prev = line > 0
     has_next = line < groups - 1
     has_next2 = line < groups - 2
-    back_line = jnp.where(x == 0, line + 3, line - 1)
-    back_from = jnp.where(x == 3, line - 3, line + 1)
+    back_line = jnp.where(x == 1, line - 1, line + 3)
+    back_from = jnp.where(x == 0, line + 1, line - 3)
     has_back = jnp.logical_and(back_from >= 0, back_from < groups - 2)
 
     def w_copy(c):
@@ -107,7 +107,7 @@
         greet_line(back_from + 2)
 
     old_x = (line + 2) % 4
-    old_relay = jnp.where(old_x == 0, line + 1, line - 3)
+    old_relay = jnp.where(old_x == 1, line - 3, line + 1)
 
     @pl.when(line >= 2)
     def _():

time: 120 us -> 104 us (0.87)
  the two profiles are of different devices: /device:TPU:8 before, /device:TPU:24 now
where the time goes in v3:
time: 104 us
  Pallas kernels  100 us (96%)
  local copies, waits for them, and re-layouts  3.4 us (3%)
    pallas_call x1, Pallas kernels, shards(): pl.pallas_call(functools.partial(kernel, groups), out_shape=jax.ShapeDtyp...  100 us
    unnamed x2, local copies, waits for them, and re-layouts  3.4 us

profile of v3, /device:TPU:24, one launch (start us, length us, event | category | flops | bytes accessed | tf_op | source)
XLA Modules:
  0.0 104.3 jit_solution(296958694903427430)
XLA Ops:
  0.7 1.3 %copy.9.mod = f32[1,3,1536]{2,1,0:T(4,128)} copy(f32[1,3,1536]{2,0,1:T(1,128)} %param.9) | data formatting | bytes 36864 | tf_op args[1]
  2.0 100.2 %shard_map.82 = bf16[256,1536]{1,0:T(8,128)(2,1)} custom-call(bf16[256,1536]{1,0:T(8,128)(2,1)} %tokens.1, f32[1,3,1536]{2,1,0:T(4,128)} %copy.9.mod, bf16[3,1536,768]{2,1,0:T(8,128)(2,1)} %w_hbm.1, bf16[768,1536]{1,0:T(8,128)(2,1)} %ow_hbm.1, f32[2,768]{1,0:T(2,128)} %gain.1, bf16[256,1536]{1,0:T(8,128)(2,1)} %text.1, s32[1]{0:T(128)S(6)} %copy.11.count, ...), custom_call_target="tpu_custom_call" | custom-call | flops 12999999488 | bytes 12000000 | tf_op jit(solution)/shard_map/pallas_call | solution.py:585
  102.2 2.1 %copy.12 = bf16[256,1536]{1,0:T(8,128)(2,1)} copy(bf16[256,1536]{1,0:T(8,128)(2,1)} %shard_map.82) | data formatting | bytes 1572864

commit v4 on v3

--- a/solution.py
+++ b/solution.py
@@ -227,7 +227,7 @@
         return p, h, part
 
     def by_next(k):
-        return jnp.logical_and(k < 4, k % 2 == 0)
+        return jnp.logical_and(k >= 4, k % 2 == 0)
 
     def own_goes(k, o):
         return has_next, jnp.logical_and(jnp.logical_and(has_next2, o > 0), jnp.logical_not(by_next(k))), core == 0
@@ -248,7 +248,7 @@
         p = subs[0][0]
         o = 2 * core + p
         for _, h, part in subs:
-            @pl.when(jnp.logical_or(jnp.logical_not(near), kk > 0))
+            @pl.when(jnp.logical_or(jnp.logical_not(near), kk == 1))
             def _():
                 hid_wait(p, h, part)
 
@@ -277,7 +277,7 @@
             lanes = slice(hd * HEAD_DIM, (hd + 1) * HEAD_DIM)
             normed = head_norm(queries[:, lanes], 0, hd)
             for n, (_, h, part) in enumerate(subs):
-                q[p, hd, sub_rows(h, part), :] = normed[n * half:(n + 1) * half]
+                q[hd, sub_rows(2 * p + h, part), :] = normed[n * half:(n + 1) * half]
         return carry
 
     def pass_sub(k, carry):
@@ -314,12 +314,23 @@
         tk[hd] = head_norm(text_keys[:, lanes], 1, hd)
         tk[GROUP + hd] = text_values[:, lanes].astype(jnp.bfloat16)
 
-    lax.fori_loop(0, 2, pass_sub, 0)
+    lax.fori_loop(0, 4, pass_sub, 0)
+
+    @pl.when(jnp.logical_not(near))
+    def _():
+        for p in range(2):
+            for h in range(2):
+                hid_pass(p, h).wait_send()
+
+    @pl.when(near)
+    def _():
+        for k in range(4, 8):
+            hid_wait(*sub_of(k))
+
     hid_copy(0, 0).wait_send()
     hid_copy(1, 1).wait_send()
     hid_copy(0, 1).start()
     hid_copy(1, 0).start()
-    lax.fori_loop(2, 4, pass_sub, 0)
     lax.fori_loop(2, 4, own_pair, 0)
 
     piece_rows = width // 2 // (2 * depth)
@@ -349,75 +360,75 @@
             ow_send.at[depth + d], ow_recv.at[n], beside,
         )
 
+
+    @pl.when(near)
+    def _():
+        win_copy(0).wait_send()
+
+    @pl.when(jnp.logical_not(near))
+    def _():
+        win_copy(0).wait_send()
+        win_copy(1).wait_send()
+
+    def win_wait(p):
+        remote(win_mine, win.at[p], win_send.at[0], win_recv.at[p], beside).wait_recv()
+
+    @pl.when(near)
+    def _():
+        win_wait(partner)
+
+    @pl.when(jnp.logical_not(near))
+    def _():
+        win_wait(0)
+        win_wait(1)
+
+    def attend(keys, values, spans, text_keys=False):
+        first, size = spans[0][0] * 2 * rows, 2 * rows
+        at = slice(first, first + len(spans) * size)
+        for hd in range(GROUP):
+            s = dot_t(q[hd, at, :], keys(hd))
+            if text_keys:
+                s = jnp.where(lax.broadcasted_iota(jnp.int32, s.shape, 1) < count[0], s, LOW)
+            weights, shrinks = [], []
+            for n, (p, low) in enumerate(spans):
+                mine_at = slice(p * size, (p + 1) * size)
+                part = s[n * size:(n + 1) * size]
+                m = jnp.broadcast_to(jnp.max(part, axis=1, keepdims=True) * SCALE, (size, HEAD_DIM))
+                if not text_keys:
+                    before = top[hd, mine_at, :]
+                    m = jnp.maximum(before, m + low)
+                    shrink = jnp.exp2(before - m)
+                    shrinks.append(shrink)
+                top[hd, mine_at, :] = m
+                if not text_keys:
+                    m = m - low
+                e = [jnp.exp2(part[:, c:c + HEAD_DIM] * SCALE - m) for c in range(0, s.shape[1], HEAD_DIM)]
+                total = functools.reduce(jnp.add, e)
+                tot[hd, mine_at, :] = total if text_keys else tot[hd, mine_at, :] * shrink + total
+                weights.append(jnp.concatenate([v.astype(jnp.bfloat16) for v in e], axis=1))
+            summed = dot(jnp.concatenate(weights, axis=0), values(hd))
+            acc[hd, at, :] = summed if text_keys else acc[hd, at, :] * jnp.concatenate(shrinks, axis=0) + summed
+
+    def text_attend():
+        attend(lambda hd: tk[hd], lambda hd: tk[GROUP + hd], [(0, 0.0), (1, 0.0)], text_keys=True)
+
+    def frame_attend(g, o, ps=(0, 1)):
+        frame = (4 * (line - 2) + 4 * g + o).astype(jnp.float32)
+
+        def low(p):
+            inside = jnp.logical_and(frame >= win[p, 0, :1], frame < win[p, 1, :1])
+            return jnp.where(inside, 0.0, LOW)
+
+        attend(lambda hd: kv[g, o, hd], lambda hd: kv[g, o, GROUP + hd], [(p, low(p)) for p in ps])
+
+    text_attend()
+    lax.fori_loop(4, 6, pass_sub, 0)
+    frame_attend(2, 2 * core)
+    pass_sub(6, 0)
+    frame_attend(2, 2 * core + 1, (1,))
+    pass_sub(7, 0)
     ow_copy().wait()
     ow_cross().start()
-
-    @pl.when(near)
-    def _():
-        win_copy(0).wait_send()
-
-    @pl.when(jnp.logical_not(near))
-    def _():
-        win_copy(0).wait_send()
-        win_copy(1).wait_send()
-
-    def win_wait(p):
-        remote(win_mine, win.at[p], win_send.at[0], win_recv.at[p], beside).wait_recv()
-
-    @pl.when(near)
-    def _():
-        win_wait(partner)
-
-    @pl.when(jnp.logical_not(near))
-    def _():
-        win_wait(0)
-        win_wait(1)
-
-    def text_attend(t, carry):
-        p, hd = t // GROUP, t % GROUP
-        s = dot_t(q[p, hd], tk[hd])
-        s = jnp.where(lax.broadcasted_iota(jnp.int32, s.shape, 1) < count[0], s, LOW)
-        m = jnp.broadcast_to(jnp.max(s, axis=1, keepdims=True) * SCALE, (2 * rows, HEAD_DIM))
-        e = [jnp.exp2(s[:, n:n + HEAD_DIM] * SCALE - m) for n in range(0, s.shape[1], HEAD_DIM)]
-        top[p, hd] = m
-        tot[p, hd] = functools.reduce(jnp.add, e)
-        acc[p, hd] = dot(jnp.concatenate([v.astype(jnp.bfloat16) for v in e], axis=1), tk[GROUP + hd])
-        return carry
-
-    def frame_attend(g, o):
-        frame = (4 * (line - 2) + 4 * g + o).astype(jnp.float32)
-
-        def step(t, carry):
-            p, hd = t // GROUP, t % GROUP
-            inside = jnp.logical_and(frame >= win[p, 0, :1], frame < win[p, 1, :1])
-            s = dot_t(q[p, hd], kv[g, o, hd])
-            m = jnp.broadcast_to(jnp.max(s, axis=1, keepdims=True) * SCALE, (2 * rows, HEAD_DIM))
-            before = top[p, hd]
-            m = jnp.maximum(before, jnp.where(inside, m, LOW))
-            top[p, hd] = m
-            shrink = jnp.exp2(before - m)
-            m = jnp.where(inside, m, -LOW)
-            e = [jnp.exp2(s[:, n:n + HEAD_DIM] * SCALE - m) for n in range(0, s.shape[1], HEAD_DIM)]
-            tot[p, hd] = tot[p, hd] * shrink + functools.reduce(jnp.add, e)
-            acc[p, hd] = acc[p, hd] * shrink + dot(
-                jnp.concatenate([v.astype(jnp.bfloat16) for v in e], axis=1), kv[g, o, GROUP + hd]
-            )
-            return carry
-
-        return step
-
-    lax.fori_loop(0, 2 * GROUP, text_attend, 0)
-    pass_sub(4, 0)
-    lax.fori_loop(0, GROUP, frame_attend(2, 2 * core), 0)
-    pass_sub(5, 0)
-    lax.fori_loop(GROUP, 2 * GROUP, frame_attend(2, 2 * core), 0)
-    pass_sub(6, 0)
-    lax.fori_loop(GROUP, 2 * GROUP, frame_attend(2, 2 * core + 1), 0)
-    pass_sub(7, 0)
-
-    def slot(j):
-        s = 1 + 2 * core + j
-        return s // 4, s % 4
 
     def slot_wait(g, o):
         for n in range(4):
@@ -429,15 +440,17 @@
                 old_share(h, part).start()
 
     def newer(i, carry):
-        g, o = slot(6 - i)
-
-        @pl.when(jnp.logical_and(g > 0, line + g >= 2))
+        kind = jnp.where(near, i // 2, (i // 2 + 1) % 3)
+        g = jnp.where(kind == 1, 2, 1)
+        o = 2 * jnp.where(kind == 0, core, partner) + 1 - i % 2
+
+        @pl.when(jnp.where(kind == 1, core == 1, has_prev))
         def _():
-            @pl.when(jnp.logical_or(g != 1, o // 2 != core))
+            @pl.when(kind != 0)
             def _():
                 slot_wait(g, o)
 
-            lax.fori_loop(0, 2 * GROUP, frame_attend(g, o), 0)
+            frame_attend(g, o)
 
         return carry
 
@@ -459,8 +472,9 @@
     def finish(p):
         for hd in range(GROUP):
             lanes = slice(hd * HEAD_DIM, (hd + 1) * HEAD_DIM)
-            total = jnp.sum(tot[p, hd], axis=1, keepdims=True)
-            result = (acc[p, hd] / total).astype(jnp.bfloat16)
+            at = slice(p * 2 * rows, (p + 1) * 2 * rows)
+            total = jnp.sum(tot[hd, at, :], axis=1, keepdims=True)
+            result = (acc[hd, at, :] / total).astype(jnp.bfloat16)
             for h in range(2):
                 att[p, h, :, lanes] = result[h * rows:(h + 1) * rows]
         for h in range(2):
@@ -474,25 +488,22 @@
             def _():
                 attin[z] = att[p, h]
 
-    for j in (2, 1):
-        @pl.when(jnp.logical_and(line >= 2, core == 0))
-        def _():
-            g, o = 0, 1 + j
-            slot_wait(g, o)
-            lax.fori_loop(GROUP, 2 * GROUP, frame_attend(g, o), 0)
+    @pl.when(jnp.logical_and(line >= 2, core == 0))
+    def _():
+        def oldest(n, carry):
+            slot_wait(0, 3 - n)
+            frame_attend(0, 3 - n)
+            return carry
+
+        lax.fori_loop(0, 2, oldest, 0)
 
     finish(1)
 
-    @pl.when(jnp.logical_and(line >= 2, core == 0))
-    def _():
-        slot_wait(0, 1)
-        for o in (3, 2, 1):
-            lax.fori_loop(0, GROUP, frame_attend(0, o), 0)
-
-    @pl.when(jnp.logical_and(line >= 2, core == 1))
-    def _():
-        slot_wait(0, 3)
-        lax.fori_loop(0, GROUP, frame_attend(0, 3), 0)
+    @pl.when(line >= 2)
+    def _():
+        o = jnp.where(core == 0, 1, 3)
+        slot_wait(0, o)
+        frame_attend(0, o, (0,))
 
     finish(0)
 
@@ -530,9 +541,6 @@
     def _():
         hid_copy(2, 0).wait_send()
         hid_copy(2, 1).wait_send()
-        for p in range(2):
-            for h in range(2):
-                hid_pass(p, h).wait_send()
 
     ow_cross().wait_send()
     for d in range(1, depth):
@@ -596,10 +604,10 @@
             pltpu.VMEM((2, width // 2, width), bf16),
             pltpu.VMEM((4, 4, 2 * GROUP, 2 * rows, HEAD_DIM), bf16),
             pltpu.VMEM((2 * GROUP, text_rows, HEAD_DIM), bf16),
-            pltpu.VMEM((2, GROUP, 2 * rows, HEAD_DIM), bf16),
-            pltpu.VMEM((2, GROUP, 2 * rows, HEAD_DIM), f32),
-            pltpu.VMEM((2, GROUP, 2 * rows, HEAD_DIM), f32),
-            pltpu.VMEM((2, GROUP, 2 * rows, HEAD_DIM), f32),
+            pltpu.VMEM((GROUP, 4 * rows, HEAD_DIM), bf16),
+            pltpu.VMEM((GROUP, 4 * rows, HEAD_DIM), f32),
+            pltpu.VMEM((GROUP, 4 * rows, HEAD_DIM), f32),
+            pltpu.VMEM((GROUP, 4 * rows, HEAD_DIM), f32),
             pltpu.VMEM((2, 2, rows, cols), bf16),
             pltpu.VMEM((4, rows, cols), bf16),
             dma((4,)),

time: 104 us -> 93.6 us (0.90)
  Pallas kernels: 100 us -> 89.3 us
    pallas_call x1, Pallas kernels: 100 us -> 89.3 us  [shards(): pl.pallas_call(functools.partial(kernel, groups), out_shape=jax.ShapeDtyp...]
where the time goes in v4:
time: 93.6 us; the launch traced here: 93.4 us
  Pallas kernels  89.3 us (95%)
  local copies, waits for them, and re-layouts  3.4 us (4%)
    pallas_call x1, Pallas kernels, shards(): pl.pallas_call(functools.partial(kernel, groups), out_shape=jax.ShapeDtyp...  89.3 us
    unnamed x2, local copies, waits for them, and re-layouts  3.4 us

profile of v4, /device:TPU:24, one launch (start us, length us, event | category | flops | bytes accessed | tf_op | source)
XLA Modules:
  0.0 93.4 jit_solution(13413107866474532345)
XLA Ops:
  0.7 1.3 %copy.9.mod = f32[1,3,1536]{2,1,0:T(4,128)} copy(f32[1,3,1536]{2,0,1:T(1,128)} %param.9) | data formatting | bytes 36864 | tf_op args[1]
  2.0 89.3 %shard_map.82 = bf16[256,1536]{1,0:T(8,128)(2,1)} custom-call(bf16[256,1536]{1,0:T(8,128)(2,1)} %tokens.1, f32[1,3,1536]{2,1,0:T(4,128)} %copy.9.mod, bf16[3,1536,768]{2,1,0:T(8,128)(2,1)} %w_hbm.1, bf16[768,1536]{1,0:T(8,128)(2,1)} %ow_hbm.1, f32[2,768]{1,0:T(2,128)} %gain.1, bf16[256,1536]{1,0:T(8,128)(2,1)} %text.1, s32[1]{0:T(128)S(6)} %copy.11.count, ...), custom_call_target="tpu_custom_call" | custom-call | flops 12999999488 | bytes 12000000 | tf_op jit(solution)/shard_map/pallas_call | solution.py:593
  91.3 2.1 %copy.12 = bf16[256,1536]{1,0:T(8,128)(2,1)} copy(bf16[256,1536]{1,0:T(8,128)(2,1)} %shard_map.82) | data formatting | bytes 1572864

commit v5 on v4

--- a/solution.py
+++ b/solution.py
@@ -27,7 +27,7 @@
     groups,
     tokens, mod, w_hbm, ow_hbm, gain, text, count, window,
     out,
-    mine, hid, win_mine, win, w, ow, kv, tk, q, acc, top, tot, att, attin,
+    hid, win_mine, win, w, ow, kv, tk, q, acc, top, tot, att, attin,
     w_sem, hid_send, hid_relay, hid_recv, win_send, win_recv, kv_send, kv_recv, ow_send, ow_recv, att_send, att_recv,
 ):
     rows, width = tokens.shape
@@ -43,7 +43,7 @@
     core = fi % 2
     z = 2 * tok + zlo
     partner = 1 - core
-    near = core == zlo
+    a_late, a_soon = zlo, 1 - zlo
 
     def dev(line_, z_, core_):
         return (4 * line_ + 2 * (z_ % 2) + core_, z_ // 2)
@@ -128,7 +128,7 @@
         v = v - jnp.mean(v, axis=-1, keepdims=True)
         spread = jnp.mean(v * v, axis=-1, keepdims=True)
         v = v * lax.rsqrt(spread + EPSILON)
-        mine[at, :] = (v * (1.0 + mod[0, 1:2, :]) + mod[0, 0:1, :]).astype(jnp.bfloat16)
+        hid[zlo, tok, at, :] = (v * (1.0 + mod[0, 1:2, :]) + mod[0, 0:1, :]).astype(jnp.bfloat16)
         return carry
 
     lax.fori_loop(0, rows // step_rows, norm_rows, 0)
@@ -140,48 +140,38 @@
     def half_at(part):
         return pl.ds(pl.multiple_of(part * half, half), half)
 
-    def hid_copy(which, part):
-        device = (dev(line, (z + 1) % 4, zlo), dev(line, (z + 3) % 4, zlo), dev(line, z, zlo))[which]
+    half_below = ((z + 3) % 4) // 2
+    half_above = ((z + 1) % 4) // 2
+
+    def hid_copy(up, part):
+        at = half_at(part)
         return remote(
-            mine.at[half_at(part), :], hid.at[core, tok, half_at(part), :],
-            hid_send.at[which, part], hid_recv.at[core, tok, part], device,
-        )
-
-    def win_copy(which):
-        device = (dev(line, (z + 1) % 4, zlo), dev(line, z, zlo))[which]
-        return remote(win_mine, win.at[core], win_send.at[which], win_recv.at[core], device)
-
-    def hid_wait(p, h, part):
+            hid.at[zlo, tok, at, :], hid.at[zlo, tok, at, :],
+            hid_send.at[up, part], hid_recv.at[zlo, tok, part], dev(line, (z + (1 if up else 3)) % 4, core),
+        )
+
+    win_copy = remote(win_mine, win.at[zlo], win_send, win_recv, dev(line, (z + 1) % 4, core))
+
+    def hid_wait(a, h, part):
+        at = half_at(part)
         remote(
-            mine.at[half_at(part), :], hid.at[p, h, half_at(part), :],
-            hid_send.at[0, part], hid_recv.at[p, h, part], beside,
+            hid.at[a, h, at, :], hid.at[a, h, at, :], hid_send.at[0, part], hid_recv.at[a, h, part], beside
         ).wait_recv()
 
-    def first_part(h):
-        return jnp.where((2 * h + core + 1) % 4 == z, 0, 1)
-
-    def hid_pass(p, h):
-        part = first_part(h)
+    def hid_pass(up):
+        h, part = (half_below, 0) if up else (half_above, 1)
+        at = half_at(part)
         return remote(
-            hid.at[p, h, half_at(part), :], hid.at[p, h, half_at(part), :],
-            hid_relay.at[p, h], hid_recv.at[p, h, part], dev(line, (z + 1 + 2 * part) % 4, core),
-        )
-
+            hid.at[a_soon, h, at, :], hid.at[a_soon, h, at, :],
+            hid_relay.at[up], hid_recv.at[a_soon, h, part], dev(line, (z + (1 if up else 3)) % 4, core),
+        )
+
+    hid_copy(1, 0).start()
+    hid_copy(0, 1).start()
+    hid_copy(1, 1).start()
     hid_copy(0, 0).start()
-    hid_copy(1, 1).start()
-
-    @pl.when(jnp.logical_not(near))
-    def _():
-        hid_copy(2, 0).start()
-        hid_copy(2, 1).start()
-        win_copy(1).start()
-
-    win_copy(0).start()
-
-    @pl.when(near)
-    def _():
-        hid[core, tok] = mine[...]
-        win[core] = win_mine[...]
+    win_copy.start()
+    win[zlo] = win_mine[...]
 
     def sub_rows(h, part):
         return pl.ds(pl.multiple_of((2 * h + part) * half, half), half)
@@ -218,19 +208,21 @@
         return kv_copy(5, 3, o, h, part, 0, dev(back_from + 2, z, old_core(o)))
 
     def old_share(h, part):
-        return kv_copy(6, 0, 3, h, part, 0, beside)
+        return kv_copy(6, 0, 2 + core, h, part, 0, beside)
 
     def sub_of(k):
-        h = jnp.where(near, (tok + k // 4) % 2, k % 2)
-        p = jnp.where(near, (core + k // 2) % 2, (k // 2) % 2)
-        part = jnp.where(near, k % 2, (first_part(h) + k // 4) % 2)
-        return p, h, part
+        kk, e = k // 2, k % 2
+        outer = jnp.logical_or(kk == 0, kk == 3)
+        a = jnp.where(outer, a_late, a_soon)
+        h = jnp.where(outer, (tok + kk // 3) % 2, jnp.where(e == 0, half_below, half_above))
+        part = jnp.where(kk == 2, 1 - e, e)
+        return a, h, part
 
     def by_next(k):
-        return jnp.logical_and(k >= 4, k % 2 == 0)
+        return k == 2
 
     def own_goes(k, o):
-        return has_next, jnp.logical_and(jnp.logical_and(has_next2, o > 0), jnp.logical_not(by_next(k))), core == 0
+        return has_next, jnp.logical_and(jnp.logical_and(has_next2, o > 0), jnp.logical_not(by_next(k))), o < 3
 
     def pass_goes(k, o):
         return (
@@ -246,15 +238,15 @@
     def own_pair(kk, carry):
         subs = [sub_of(2 * kk), sub_of(2 * kk + 1)]
         p = subs[0][0]
-        o = 2 * core + p
-        for _, h, part in subs:
-            @pl.when(jnp.logical_or(jnp.logical_not(near), kk == 1))
-            def _():
+        o = 2 * p + core
+        @pl.when(kk > 0)
+        def _():
+            for n, (_, h, part) in enumerate(subs):
                 hid_wait(p, h, part)
 
-                @pl.when(jnp.logical_and(jnp.logical_not(near), kk < 2))
+                @pl.when(kk == 1)
                 def _():
-                    hid_pass(p, h).start()
+                    hid_pass(1 - n).start()
 
         v = jnp.concatenate([hid[p, h, half_at(part), :] for _, h, part in subs], axis=0)
         keys = dot(v, w[1])
@@ -282,8 +274,13 @@
 
     def pass_sub(k, carry):
         p, h, part = sub_of(k)
-        o = 2 * core + p
+        o = 2 * p + core
         go_next, go_back = pass_goes(k, o)
+
+        @pl.when(go_back)
+        def _():
+            kv_wait(3, o, h, part)
+            pass_back(o, h, part).start()
 
         @pl.when(has_prev)
         def _():
@@ -295,17 +292,12 @@
 
             pass_share(o, h, part).start()
 
-        @pl.when(go_back)
-        def _():
-            kv_wait(3, o, h, part)
-            pass_back(o, h, part).start()
-
         return carry
 
     for c in (1, 2, 0):
         w_copy(c).wait()
     ow_copy().start()
-    lax.fori_loop(0, 2, own_pair, 0)
+    lax.fori_loop(0, 1, own_pair, 0)
 
     text_keys = dot(text[...], w[1])
     text_values = dot(text[...], w[2])
@@ -314,24 +306,10 @@
         tk[hd] = head_norm(text_keys[:, lanes], 1, hd)
         tk[GROUP + hd] = text_values[:, lanes].astype(jnp.bfloat16)
 
-    lax.fori_loop(0, 4, pass_sub, 0)
-
-    @pl.when(jnp.logical_not(near))
-    def _():
-        for p in range(2):
-            for h in range(2):
-                hid_pass(p, h).wait_send()
-
-    @pl.when(near)
-    def _():
-        for k in range(4, 8):
-            hid_wait(*sub_of(k))
-
-    hid_copy(0, 0).wait_send()
-    hid_copy(1, 1).wait_send()
-    hid_copy(0, 1).start()
-    hid_copy(1, 0).start()
-    lax.fori_loop(2, 4, own_pair, 0)
+    lax.fori_loop(0, 2, pass_sub, 0)
+    lax.fori_loop(1, 2, own_pair, 0)
+    lax.fori_loop(2, 4, pass_sub, 0)
+    lax.fori_loop(2, 3, own_pair, 0)
 
     piece_rows = width // 2 // (2 * depth)
 
@@ -361,113 +339,144 @@
         )
 
 
-    @pl.when(near)
-    def _():
-        win_copy(0).wait_send()
-
-    @pl.when(jnp.logical_not(near))
-    def _():
-        win_copy(0).wait_send()
-        win_copy(1).wait_send()
-
-    def win_wait(p):
-        remote(win_mine, win.at[p], win_send.at[0], win_recv.at[p], beside).wait_recv()
-
-    @pl.when(near)
-    def _():
-        win_wait(partner)
-
-    @pl.when(jnp.logical_not(near))
-    def _():
-        win_wait(0)
-        win_wait(1)
+    win_copy.wait()
+
+    size = 2 * rows
 
     def attend(keys, values, spans, text_keys=False):
-        first, size = spans[0][0] * 2 * rows, 2 * rows
-        at = slice(first, first + len(spans) * size)
+        ats = [pl.ds(pl.multiple_of(a * size, size), size) for a, _ in spans]
         for hd in range(GROUP):
-            s = dot_t(q[hd, at, :], keys(hd))
+            s = dot_t(jnp.concatenate([q[hd, at, :] for at in ats], axis=0), keys(hd))
             if text_keys:
                 s = jnp.where(lax.broadcasted_iota(jnp.int32, s.shape, 1) < count[0], s, LOW)
             weights, shrinks = [], []
-            for n, (p, low) in enumerate(spans):
-                mine_at = slice(p * size, (p + 1) * size)
+            for n, (_, low) in enumerate(spans):
                 part = s[n * size:(n + 1) * size]
                 m = jnp.broadcast_to(jnp.max(part, axis=1, keepdims=True) * SCALE, (size, HEAD_DIM))
                 if not text_keys:
-                    before = top[hd, mine_at, :]
+                    before = top[hd, ats[n], :]
                     m = jnp.maximum(before, m + low)
-                    shrink = jnp.exp2(before - m)
-                    shrinks.append(shrink)
-                top[hd, mine_at, :] = m
+                    shrinks.append(jnp.exp2(before - m))
+                top[hd, ats[n], :] = m
                 if not text_keys:
                     m = m - low
                 e = [jnp.exp2(part[:, c:c + HEAD_DIM] * SCALE - m) for c in range(0, s.shape[1], HEAD_DIM)]
                 total = functools.reduce(jnp.add, e)
-                tot[hd, mine_at, :] = total if text_keys else tot[hd, mine_at, :] * shrink + total
+                tot[hd, ats[n], :] = total if text_keys else tot[hd, ats[n], :] * shrinks[n] + total
                 weights.append(jnp.concatenate([v.astype(jnp.bfloat16) for v in e], axis=1))
             summed = dot(jnp.concatenate(weights, axis=0), values(hd))
-            acc[hd, at, :] = summed if text_keys else acc[hd, at, :] * jnp.concatenate(shrinks, axis=0) + summed
-
-    def text_attend():
-        attend(lambda hd: tk[hd], lambda hd: tk[GROUP + hd], [(0, 0.0), (1, 0.0)], text_keys=True)
-
-    def frame_attend(g, o, ps=(0, 1)):
+            for n, at in enumerate(ats):
+                part = summed[n * size:(n + 1) * size]
+                acc[hd, at, :] = part if text_keys else acc[hd, at, :] * shrinks[n] + part
+
+    def text_attend(a):
+        attend(lambda hd: tk[hd], lambda hd: tk[GROUP + hd], [(a, 0.0)], text_keys=True)
+
+    def frame_attend(g, o, *queries):
         frame = (4 * (line - 2) + 4 * g + o).astype(jnp.float32)
 
-        def low(p):
-            inside = jnp.logical_and(frame >= win[p, 0, :1], frame < win[p, 1, :1])
+        def low(a):
+            inside = jnp.logical_and(frame >= win[a, 0, :1], frame < win[a, 1, :1])
             return jnp.where(inside, 0.0, LOW)
 
-        attend(lambda hd: kv[g, o, hd], lambda hd: kv[g, o, GROUP + hd], [(p, low(p)) for p in ps])
-
-    text_attend()
-    lax.fori_loop(4, 6, pass_sub, 0)
-    frame_attend(2, 2 * core)
-    pass_sub(6, 0)
-    frame_attend(2, 2 * core + 1, (1,))
-    pass_sub(7, 0)
+        attend(lambda hd: kv[g, o, hd], lambda hd: kv[g, o, GROUP + hd], [(a, low(a)) for a in queries])
+
+    def frame_wait(g, o):
+        for n in range(4):
+            kv_wait(g, o, n // 2, n % 2)
+
+    def shared(i):
+        return 2 * i + partner < 3
+
+    def soon(i):
+        return jnp.where(i < 2, 2, 1), 2 * a_soon + (core + i) % 2
+
+    def late(i):
+        return jnp.where(i < 2, 2, 1), 2 * a_late + (core + i) % 2
+
+    def reaches(g, o, a):
+        return jnp.where(g == 2, o <= 2 * a + core, has_prev)
+
+    text_attend(a_soon)
+
+    def first(i, carry):
+        g, o = soon(i)
+
+        @pl.when(i == 2)
+        def _():
+            pass_sub(4, 0)
+            pass_sub(5, 0)
+
+        @pl.when(jnp.logical_or(jnp.logical_and(i == 1, shared(a_soon)), jnp.logical_and(i == 3, has_prev)))
+        def _():
+            frame_wait(g, o)
+
+        @pl.when(reaches(g, o, a_soon))
+        def _():
+            frame_attend(g, o, a_soon)
+
+        return carry
+
+    lax.fori_loop(0, 4, first, 0)
+    lax.fori_loop(3, 4, own_pair, 0)
     ow_copy().wait()
     ow_cross().start()
-
-    def slot_wait(g, o):
-        for n in range(4):
-            h, part = n // 2, n % 2
-            kv_wait(g, o, h, part)
-
-            @pl.when(jnp.logical_and(g == 0, core == 1))
-            def _():
-                old_share(h, part).start()
-
-    def newer(i, carry):
-        kind = jnp.where(near, i // 2, (i // 2 + 1) % 3)
-        g = jnp.where(kind == 1, 2, 1)
-        o = 2 * jnp.where(kind == 0, core, partner) + 1 - i % 2
-
-        @pl.when(jnp.where(kind == 1, core == 1, has_prev))
-        def _():
-            @pl.when(kind != 0)
-            def _():
-                slot_wait(g, o)
-
-            frame_attend(g, o)
-
-        return carry
-
-    lax.fori_loop(0, 6, newer, 0)
-
+    text_attend(a_late)
+
+    def second(i, carry):
+        g_soon, o_soon = soon(i)
+        _, o_late = late(i % 2)
+        early = i < 4
+        g = jnp.where(early, g_soon, 2)
+        o = jnp.where(early, o_soon, o_late)
+        a = jnp.where(i < 6, a_late, a_soon)
+
+        @pl.when(i == 5)
+        def _():
+            pass_sub(6, 0)
+
+        @pl.when(i == 7)
+        def _():
+            pass_sub(7, 0)
+
+        @pl.when(jnp.logical_and(i == 5, shared(a_late)))
+        def _():
+            frame_wait(g, o)
+
+        @pl.when(reaches(g, o, a))
+        def _():
+            frame_attend(g, o, a)
+
+        return carry
+
+    lax.fori_loop(0, 8, second, 0)
     ow_cross(1 - tok).wait_recv()
     for d in range(1, depth):
         ow_along(d).start()
     ow_share(0, core).start()
 
+    def third(i, carry):
+        g, o = late(i)
+
+        @pl.when(has_prev)
+        def _():
+            @pl.when(i == 3)
+            def _():
+                frame_wait(g, o)
+
+            frame_attend(g, o, 0, 1)
+
+        return carry
+
+    lax.fori_loop(2, 4, third, 0)
+
     def att_copy(p, h):
         return remote(
-            att.at[p, h], attin.at[z], att_send.at[p, h], att_recv.at[z], dev(line, 2 * h + core, p)
+            att.at[p, h], attin.at[z], att_send.at[p, h], att_recv.at[z], dev(line, 2 * h + p, core)
         )
 
     def is_here(p, h):
-        return jnp.logical_and(2 * h + core == z, p == core)
+        return 2 * h + p == z
 
     def finish(p):
         for hd in range(GROUP):
@@ -488,22 +497,34 @@
             def _():
                 attin[z] = att[p, h]
 
-    @pl.when(jnp.logical_and(line >= 2, core == 0))
-    def _():
-        def oldest(n, carry):
-            slot_wait(0, 3 - n)
-            frame_attend(0, 3 - n)
-            return carry
-
-        lax.fori_loop(0, 2, oldest, 0)
-
-    finish(1)
-
-    @pl.when(line >= 2)
-    def _():
-        o = jnp.where(core == 0, 1, 3)
-        slot_wait(0, o)
-        frame_attend(0, o, (0,))
+    has_old = line >= 2
+
+    @pl.when(core == 1)
+    def _():
+        finish(1)
+
+    @pl.when(has_old)
+    def _():
+        for n in range(4):
+            h, part = n // 2, n % 2
+            kv_wait(0, 2 + core, h, part)
+            old_share(h, part).start()
+        frame_attend(0, 2 + core, 0)
+
+    @pl.when(jnp.logical_and(has_old, core == 0))
+    def _():
+        frame_wait(0, 3)
+        frame_attend(0, 3, 0, 1)
+
+    @pl.when(core == 0)
+    def _():
+        finish(1)
+
+    @pl.when(has_old)
+    def _():
+        o = 1 + core
+        frame_wait(0, o)
+        frame_attend(0, o, 0)
 
     finish(0)
 
@@ -517,7 +538,7 @@
         ow_share(d, partner).wait_recv()
 
     for s in range(4):
-        @pl.when(jnp.logical_not(jnp.logical_and(s == z, near)))
+        @pl.when(s != z)
         def _():
             remote(att.at[0, 0], attin.at[s], att_send.at[0, 0], att_recv.at[s], beside).wait_recv()
 
@@ -534,13 +555,10 @@
 
     lax.fori_loop(0, width // step_cols, project, 0)
 
-    hid_copy(0, 1).wait_send()
-    hid_copy(1, 0).wait_send()
-
-    @pl.when(jnp.logical_not(near))
-    def _():
-        hid_copy(2, 0).wait_send()
-        hid_copy(2, 1).wait_send()
+    for n in range(2):
+        hid_copy(n, 0).wait_send()
+        hid_copy(n, 1).wait_send()
+        hid_pass(n).wait_send()
 
     ow_cross().wait_send()
     for d in range(1, depth):
@@ -556,7 +574,7 @@
 
     def drain(k, carry):
         p, h, part = sub_of(k)
-        o = 2 * core + p
+        o = 2 * p + core
         for flag, copy in zip(own_goes(k, o), (own_next, own_back, own_share)):
             @pl.when(flag)
             def _():
@@ -571,7 +589,7 @@
         def _():
             pass_share(o, h, part).wait_send()
 
-        @pl.when(jnp.logical_and(jnp.logical_and(line >= 2, core == 1), p == 0))
+        @pl.when(jnp.logical_and(has_old, p == 0))
         def _():
             old_share(h, part).wait_send()
 
@@ -596,7 +614,6 @@
         in_specs=[vmem, vmem, hbm, hbm, vmem, vmem, smem, smem],
         out_specs=vmem,
         scratch_shapes=[
-            pltpu.VMEM((rows, width), bf16),
             pltpu.VMEM((2, 2, rows, width), bf16),
             pltpu.VMEM((2, 8, HEAD_DIM), f32),
             pltpu.VMEM((2, 2, 8, HEAD_DIM), f32),
@@ -611,11 +628,11 @@
             pltpu.VMEM((2, 2, rows, cols), bf16),
             pltpu.VMEM((4, rows, cols), bf16),
             dma((4,)),
-            dma((3, 2)),
             dma((2, 2)),
+            dma((2,)),
             dma((2, 2, 2)),
-            dma((2,)),
-            dma((2,)),
+            dma,
+            dma,
             dma((7, 4, 4)),
             dma((4, 4, 4)),
             dma((2 * depth,)),

time: 93.6 us -> 89.3 us (0.954)
  Pallas kernels: 89.3 us -> 85 us
    pallas_call x1, Pallas kernels: 89.3 us -> 85 us  [shards(): pl.pallas_call(functools.partial(kernel, groups), out_shape=jax.ShapeDtyp...]
where the time goes in v5:
time: 89.3 us; the launch traced here: 89.1 us
  Pallas kernels  85 us (95%)
  local copies, waits for them, and re-layouts  3.4 us (4%)
    pallas_call x1, Pallas kernels, shards(): pl.pallas_call(functools.partial(kernel, groups), out_shape=jax.ShapeDtyp...  85 us
    unnamed x2, local copies, waits for them, and re-layouts  3.4 us

profile of v5, /device:TPU:24, one launch (start us, length us, event | category | flops | bytes accessed | tf_op | source)
XLA Modules:
  0.0 89.1 jit_solution(15533665048126393617)
XLA Ops:
  0.7 1.3 %copy.9.mod = f32[1,3,1536]{2,1,0:T(4,128)} copy(f32[1,3,1536]{2,0,1:T(1,128)} %param.9) | data formatting | bytes 36864 | tf_op args[1]
  2.0 85.0 %shard_map.82 = bf16[256,1536]{1,0:T(8,128)(2,1)} custom-call(bf16[256,1536]{1,0:T(8,128)(2,1)} %tokens.1, f32[1,3,1536]{2,1,0:T(4,128)} %copy.9.mod, bf16[3,1536,768]{2,1,0:T(8,128)(2,1)} %w_hbm.1, bf16[768,1536]{1,0:T(8,128)(2,1)} %ow_hbm.1, f32[2,768]{1,0:T(2,128)} %gain.1, bf16[256,1536]{1,0:T(8,128)(2,1)} %text.1, s32[1]{0:T(128)S(6)} %copy.11.count, ...), custom_call_target="tpu_custom_call" | custom-call | flops 12999999488 | bytes 12000000 | tf_op jit(solution)/shard_map/pallas_call | solution.py:611
  87.0 2.1 %copy.12 = bf16[256,1536]{1,0:T(8,128)(2,1)} copy(bf16[256,1536]{1,0:T(8,128)(2,1)} %shard_map.82) | data formatting | bytes 1572864

commit v6 on v5

--- a/solution.py
+++ b/solution.py
@@ -219,7 +219,7 @@
         return a, h, part
 
     def by_next(k):
-        return k == 2
+        return k > 99
 
     def own_goes(k, o):
         return has_next, jnp.logical_and(jnp.logical_and(has_next2, o > 0), jnp.logical_not(by_next(k))), o < 3

time: 89.3 us -> 93.9 us (1.052)
  Pallas kernels: 85 us -> 88.8 us
    pallas_call x1, Pallas kernels: 85 us -> 88.8 us  [shards(): pl.pallas_call(functools.partial(kernel, groups), out_shape=jax.ShapeDtyp...]
where the time goes in v6:
time: 93.9 us; the launch traced here: 92.9 us
  Pallas kernels  88.8 us (95%)
  local copies, waits for them, and re-layouts  3.4 us (4%)
    pallas_call x1, Pallas kernels, shards(): pl.pallas_call(functools.partial(kernel, groups), out_shape=jax.ShapeDtyp...  88.8 us
    unnamed x2, local copies, waits for them, and re-layouts  3.4 us

profile of v6, /device:TPU:24, one launch (start us, length us, event | category | flops | bytes accessed | tf_op | source)
XLA Modules:
  0.0 92.9 jit_solution(5104623728325031860)
XLA Ops:
  0.7 1.3 %copy.9.mod = f32[1,3,1536]{2,1,0:T(4,128)} copy(f32[1,3,1536]{2,0,1:T(1,128)} %param.9) | data formatting | bytes 36864 | tf_op args[1]
  2.0 88.8 %shard_map.82 = bf16[256,1536]{1,0:T(8,128)(2,1)} custom-call(bf16[256,1536]{1,0:T(8,128)(2,1)} %tokens.1, f32[1,3,1536]{2,1,0:T(4,128)} %copy.9.mod, bf16[3,1536,768]{2,1,0:T(8,128)(2,1)} %w_hbm.1, bf16[768,1536]{1,0:T(8,128)(2,1)} %ow_hbm.1, f32[2,768]{1,0:T(2,128)} %gain.1, bf16[256,1536]{1,0:T(8,128)(2,1)} %text.1, s32[1]{0:T(128)S(6)} %copy.11.count, ...), custom_call_target="tpu_custom_call" | custom-call | flops 12999999488 | bytes 12000000 | tf_op jit(solution)/shard_map/pallas_call | solution.py:611
  90.8 2.1 %copy.12 = bf16[256,1536]{1,0:T(8,128)(2,1)} copy(bf16[256,1536]{1,0:T(8,128)(2,1)} %shard_map.82) | data formatting | bytes 1572864
